TPU v7x, 32 devices: a whole 2x2x4 slice. The times are simulated.
32 devices in a mesh: dp: 8 (over z, y), seq: 4 (over x, core).
Axes of the slice: x: 2, y: 2, z: 4, core: 2. Of those that a mesh axis runs over, the one named last changes fastest.
Arguments:
- frames: bfloat16 [8, 640, 1024], P('dp', 'seq'), may hold values from -6 to 6
- cotangent: bfloat16 [8, 640, 1024], P('dp', 'seq'), may hold values from -6 to 6
- text_states: bfloat16 [8, 256, 768], P('dp'), may hold values from -6 to 6
- frame_start: int32 [8], P('dp'), may hold values from 0 to 319
- prompt_len: int32 [8], P('dp'), may hold values from 16 to 256, as said below
- w_query: bfloat16 [1024, 1024], P(('dp', 'seq')), may hold values from -0.1875 to 0.1875
- w_key: bfloat16 [1024, 1024], P(('dp', 'seq')), may hold values from -0.1875 to 0.1875
- w_value: bfloat16 [1024, 1024], P(('dp', 'seq')), may hold values from -0.1875 to 0.1875
- w_out: bfloat16 [1024, 1024], P(('dp', 'seq')), may hold values from -1.5 to 1.5
- c_query: bfloat16 [1024, 1024], P(('dp', 'seq')), may hold values from -0.1875 to 0.1875
- c_key: bfloat16 [1024, 1024], P(('dp', 'seq')), may hold values from -0.1875 to 0.1875
- c_value: bfloat16 [1024, 1024], P(('dp', 'seq')), may hold values from -0.1875 to 0.1875
- c_out: bfloat16 [1024, 1024], P(('dp', 'seq')), may hold values from -0.5 to 0.5
- w_text: bfloat16 [768, 1024], P(('dp', 'seq')), may hold values from -0.21875 to 0.21875
- w_up: bfloat16 [1024, 4096], P(('dp', 'seq')), may hold values from -0.1875 to 0.1875
- w_down: bfloat16 [4096, 1024], P(('dp', 'seq')), may hold values from -0.09375 to 0.09375
- gain_attn: bfloat16 [1024], P(('dp', 'seq')), may hold values from 0.25 to 1.75
- bias_attn: bfloat16 [1024], P(('dp', 'seq')), may hold values from -3 to 3
- gain_cross: bfloat16 [1024], P(('dp', 'seq')), may hold values from 0.25 to 1.75
- bias_cross: bfloat16 [1024], P(('dp', 'seq')), may hold values from -3 to 3
- gain_feed: bfloat16 [1024], P(('dp', 'seq')), may hold values from 0.25 to 1.75
- bias_feed: bfloat16 [1024], P(('dp', 'seq')), may hold values from -3 to 3
Outputs:
- block_out: bfloat16 [8, 640, 1024], P('dp', 'seq')
- frames_grad: bfloat16 [8, 640, 1024], P('dp', 'seq')
- text_grad: float32 [8, 256, 768], P('dp', 'seq')
- dw_query: float32 [1024, 1024], P(('dp', 'seq'))
- dw_key: float32 [1024, 1024], P(('dp', 'seq'))
- dw_value: float32 [1024, 1024], P(('dp', 'seq'))
- dw_out: float32 [1024, 1024], P(('dp', 'seq'))
- dc_query: float32 [1024, 1024], P(('dp', 'seq'))
- dc_key: float32 [1024, 1024], P(('dp', 'seq'))
- dc_value: float32 [1024, 1024], P(('dp', 'seq'))
- dc_out: float32 [1024, 1024], P(('dp', 'seq'))
- dw_text: float32 [768, 1024], P(('dp', 'seq'))
- dw_up: float32 [1024, 4096], P(('dp', 'seq'))
- dw_down: float32 [4096, 1024], P(('dp', 'seq'))
- dgain_attn: float32 [1024], P(('dp', 'seq'))
- dbias_attn: float32 [1024], P(('dp', 'seq'))
- dgain_cross: float32 [1024], P(('dp', 'seq'))
- dbias_cross: float32 [1024], P(('dp', 'seq'))
- dgain_feed: float32 [1024], P(('dp', 'seq'))
- dbias_feed: float32 [1024], P(('dp', 'seq'))
Inputs may be any that keep to these rules, and one draw needn't show every extreme that they name: Each item's prompt holds prompt_len tokens at the front of its 256 slots; most hold 16 to 32, a few more, and some item holds exactly 256. frames before frame_start are padding: no other frame attends to them.
All inputs are finite; a program needn't handle non-finite values.
Results may differ from a plain program's by a relative error of at most 0.018.
Values may be sent and summed in bfloat16 or wider, within the bound.
A program may use at most 320 MiB of HBM per device.

v0:
```python
import jax
import jax.numpy as jnp
from jax import lax
from jax.sharding import PartitionSpec as P

HEADS = 16


eps_norm = 1e-05


def layer_norm(values_in, gain_vec, shift_vec):
    centre = values_in - jnp.mean(values_in, axis=-1, keepdims=True)
    spread = jnp.mean(centre * centre, axis=-1, keepdims=True)
    return centre * lax.rsqrt(spread + eps_norm) * gain_vec + shift_vec


def gelu_exact(values_in):
    return jax.nn.gelu(values_in, approximate=False)


def project(left, right):
    return jnp.einsum("gti,ij->gtj", left, right, preferred_element_type=jnp.float32)


def project_back(left, right):
    return jnp.einsum("gtj,ij->gti", left, right, preferred_element_type=jnp.float32)


def outer_sum(left, right):
    return jnp.einsum("gti,gtj->ij", left, right, preferred_element_type=jnp.float32)


def split_heads(rows_in):
    return rows_in.reshape(rows_in.shape[0], rows_in.shape[1], HEADS, rows_in.shape[2] // HEADS)


def merge_heads(heads_in):
    return heads_in.reshape(heads_in.shape[0], heads_in.shape[1], -1)


def softmax_rows(query_rows, key_rows, allowed):
    query_heads = split_heads(query_rows)
    key_heads = split_heads(key_rows)
    scale = query_heads.shape[3] ** (-0.5)
    scores = (
        jnp.einsum("gqhd,gkhd->ghqk", query_heads, key_heads, preferred_element_type=jnp.float32)
        * scale
    )
    scores = jnp.where(allowed[:, None], scores, -1e30)
    return jax.nn.softmax(scores, axis=-1)


def mix_values(probs_low, value_rows):
    mixture = jnp.einsum(
        "ghqk,gkhd->gqhd", probs_low, split_heads(value_rows), preferred_element_type=jnp.float32
    )
    return merge_heads(mixture).astype(jnp.bfloat16)


def attend_back(attn_probs, probs_low, query_rows, key_rows, value_rows, grad_mix):
    query_heads = split_heads(query_rows)
    key_heads = split_heads(key_rows)
    value_heads = split_heads(value_rows)
    grad_heads = split_heads(grad_mix)
    scale = query_heads.shape[3] ** (-0.5)
    grad_probs = jnp.einsum(
        "gqhd,gkhd->ghqk", grad_heads, value_heads, preferred_element_type=jnp.float32
    )
    grad_scores = attn_probs * (
        grad_probs - jnp.sum(attn_probs * grad_probs, axis=-1, keepdims=True)
    )
    scores_low = grad_scores.astype(jnp.bfloat16)
    grad_query = (
        jnp.einsum("ghqk,gkhd->gqhd", scores_low, key_heads, preferred_element_type=jnp.float32)
        * scale
    )
    grad_key = (
        jnp.einsum("ghqk,gqhd->gkhd", scores_low, query_heads, preferred_element_type=jnp.float32)
        * scale
    )
    grad_value = jnp.einsum(
        "ghqk,gqhd->gkhd", probs_low, grad_heads, preferred_element_type=jnp.float32
    )
    return (merge_heads(grad_query), merge_heads(grad_key), merge_heads(grad_value))


def on_device(
    frames,
    cotangent,
    text_states,
    frame_start,
    prompt_len,
    w_query,
    w_key,
    w_value,
    w_out,
    c_query,
    c_key,
    c_value,
    c_out,
    w_text,
    w_up,
    w_down,
    gain_attn,
    bias_attn,
    gain_cross,
    bias_cross,
    gain_feed,
    bias_feed,
):

    def attn_weights():
        return (
            lax.all_gather(w_query, ("dp", "seq"), axis=0, tiled=True),
            lax.all_gather(w_key, ("dp", "seq"), axis=0, tiled=True),
            lax.all_gather(w_value, ("dp", "seq"), axis=0, tiled=True),
            lax.all_gather(w_out, ("dp", "seq"), axis=0, tiled=True),
            lax.all_gather(c_query, ("dp", "seq"), axis=0, tiled=True),
            lax.all_gather(c_key, ("dp", "seq"), axis=0, tiled=True),
            lax.all_gather(c_value, ("dp", "seq"), axis=0, tiled=True),
            lax.all_gather(c_out, ("dp", "seq"), axis=0, tiled=True),
            lax.all_gather(w_text, ("dp", "seq"), axis=0, tiled=True),
            lax.all_gather(gain_attn, ("dp", "seq"), axis=0, tiled=True),
            lax.all_gather(bias_attn, ("dp", "seq"), axis=0, tiled=True),
            lax.all_gather(gain_cross, ("dp", "seq"), axis=0, tiled=True),
            lax.all_gather(bias_cross, ("dp", "seq"), axis=0, tiled=True),
        )

    def feed_weights():
        return (
            lax.all_gather(w_up, ("dp", "seq"), axis=0, tiled=True),
            lax.all_gather(w_down, ("dp", "seq"), axis=0, tiled=True),
            lax.all_gather(gain_feed, ("dp", "seq"), axis=0, tiled=True),
            lax.all_gather(bias_feed, ("dp", "seq"), axis=0, tiled=True),
        )

    fwd_attn = attn_weights()
    fwd_feed = feed_weights()
    (
        full_query,
        full_key,
        full_value,
        full_out,
        full_cquery,
        full_ckey,
        full_cvalue,
        full_cout,
        full_text,
        full_gain_a,
        full_bias_a,
        full_gain_c,
        full_bias_c,
    ) = fwd_attn
    full_up, full_down, full_gain_f, full_bias_f = fwd_feed
    frames_f = frames.astype(jnp.float32)
    frame_count = frames.shape[1]
    normed, norm_one_back = jax.vjp(
        layer_norm, frames_f, full_gain_a.astype(jnp.float32), full_bias_a.astype(jnp.float32)
    )
    normed_low = normed.astype(jnp.bfloat16)
    query_rows = project(normed_low, full_query).astype(jnp.bfloat16)
    key_rows = project(normed_low, full_key).astype(jnp.bfloat16)
    value_rows = project(normed_low, full_value).astype(jnp.bfloat16)
    key_all, value_all = (
        lax.all_gather(key_rows, "seq", axis=1, tiled=True),
        lax.all_gather(value_rows, "seq", axis=1, tiled=True),
    )
    rank = lax.axis_index("seq")
    query_pos = rank * frame_count + jnp.arange(frame_count)
    key_pos = jnp.arange(key_all.shape[1])
    causal = (key_pos[None, None, :] <= query_pos[None, :, None]) & (
        (key_pos[None, None, :] >= frame_start[:, None, None])
        | (key_pos[None, None, :] == query_pos[None, :, None])
    )
    attn_probs = softmax_rows(query_rows, key_all, causal)
    probs_low = attn_probs.astype(jnp.bfloat16)
    attended = mix_values(probs_low, value_all)
    first = frames_f + project(attended, full_out)
    text_count = text_states.shape[1]
    quarter = text_count // lax.axis_size("seq")
    text_start = rank * quarter
    text_part = lax.dynamic_slice_in_dim(text_states, text_start, quarter, 1)
    proj_all = project(text_states, full_text).astype(jnp.bfloat16)
    cross_keys = project(proj_all, full_ckey).astype(jnp.bfloat16)
    cross_values = project(proj_all, full_cvalue).astype(jnp.bfloat16)
    proj_part = lax.dynamic_slice_in_dim(proj_all, text_start, quarter, 1)
    normed_two, norm_two_back = jax.vjp(
        layer_norm, first, full_gain_c.astype(jnp.float32), full_bias_c.astype(jnp.float32)
    )
    normed_two_low = normed_two.astype(jnp.bfloat16)
    cross_query = project(normed_two_low, full_cquery).astype(jnp.bfloat16)
    prompt_mask = jnp.arange(text_count)[None, None, :] < prompt_len[:, None, None]
    cross_probs = softmax_rows(cross_query, cross_keys, prompt_mask)
    cross_low = cross_probs.astype(jnp.bfloat16)
    cross_mix = mix_values(cross_low, cross_values)
    second = first + project(cross_mix, full_cout)
    normed_three, norm_three_back = jax.vjp(
        layer_norm, second, full_gain_f.astype(jnp.float32), full_bias_f.astype(jnp.float32)
    )
    three_low = normed_three.astype(jnp.bfloat16)
    hidden = project(three_low, full_up)
    activated, gelu_back = jax.vjp(gelu_exact, hidden)
    act_low = activated.astype(jnp.bfloat16)
    block_out = (second + project(act_low, full_down)).astype(jnp.bfloat16)
    back_feed = feed_weights()
    back_attn = attn_weights()
    back_up = back_feed[0]
    back_down = back_feed[1]
    back_query, back_key, back_value, back_out = (
        back_attn[0],
        back_attn[1],
        back_attn[2],
        back_attn[3],
    )
    back_cquery, back_ckey, back_cvalue, back_cout = (
        back_attn[4],
        back_attn[5],
        back_attn[6],
        back_attn[7],
    )
    back_text = back_attn[8]
    grad_act = project_back(cotangent, back_down)
    dw_down = outer_sum(act_low, cotangent)
    grad_hidden = gelu_back(grad_act)[0].astype(jnp.bfloat16)
    dw_up = outer_sum(three_low, grad_hidden)
    grad_three = project_back(grad_hidden, back_up)
    grad_second_ln, dgain_feed, dbias_feed = norm_three_back(grad_three)
    grad_second = cotangent.astype(jnp.float32) + grad_second_ln
    dw_up_own, dw_down_own, dgain_feed_own, dbias_feed_own = (
        lax.psum_scatter(dw_up, ("dp", "seq"), scatter_dimension=0, tiled=True),
        lax.psum_scatter(dw_down, ("dp", "seq"), scatter_dimension=0, tiled=True),
        lax.psum_scatter(dgain_feed, ("dp", "seq"), scatter_dimension=0, tiled=True),
        lax.psum_scatter(dbias_feed, ("dp", "seq"), scatter_dimension=0, tiled=True),
    )
    second_low = grad_second.astype(jnp.bfloat16)
    dc_out = outer_sum(cross_mix, second_low)
    grad_cross_mix = project_back(second_low, back_cout).astype(jnp.bfloat16)
    grad_cq, grad_ck, grad_cv = attend_back(
        cross_probs, cross_low, cross_query, cross_keys, cross_values, grad_cross_mix
    )
    ck_summed, cv_summed = (
        lax.psum_scatter(
            grad_ck.astype(jnp.bfloat16), "seq", scatter_dimension=1, tiled=True
        ).astype(jnp.float32),
        lax.psum_scatter(
            grad_cv.astype(jnp.bfloat16), "seq", scatter_dimension=1, tiled=True
        ).astype(jnp.float32),
    )
    ck_low = ck_summed.astype(jnp.bfloat16)
    cv_low = cv_summed.astype(jnp.bfloat16)
    dc_key = outer_sum(proj_part, ck_low)
    dc_value = outer_sum(proj_part, cv_low)
    grad_proj = (project_back(ck_low, back_ckey) + project_back(cv_low, back_cvalue)).astype(
        jnp.bfloat16
    )
    dw_text = outer_sum(text_part, grad_proj)
    text_grad = project_back(grad_proj, back_text)
    cq_low = grad_cq.astype(jnp.bfloat16)
    dc_query = outer_sum(normed_two_low, cq_low)
    grad_first_ln, dgain_cross, dbias_cross = norm_two_back(project_back(cq_low, back_cquery))
    grad_first = grad_second + grad_first_ln
    (
        dc_query_own,
        dc_key_own,
        dc_value_own,
        dc_out_own,
        dw_text_own,
        dgain_cross_own,
        dbias_cross_own,
    ) = (
        lax.psum_scatter(dc_query, ("dp", "seq"), scatter_dimension=0, tiled=True),
        lax.psum_scatter(dc_key, ("dp", "seq"), scatter_dimension=0, tiled=True),
        lax.psum_scatter(dc_value, ("dp", "seq"), scatter_dimension=0, tiled=True),
        lax.psum_scatter(dc_out, ("dp", "seq"), scatter_dimension=0, tiled=True),
        lax.psum_scatter(dw_text, ("dp", "seq"), scatter_dimension=0, tiled=True),
        lax.psum_scatter(dgain_cross, ("dp", "seq"), scatter_dimension=0, tiled=True),
        lax.psum_scatter(dbias_cross, ("dp", "seq"), scatter_dimension=0, tiled=True),
    )
    first_low = grad_first.astype(jnp.bfloat16)
    dw_out = outer_sum(attended, first_low)
    grad_attended = project_back(first_low, back_out).astype(jnp.bfloat16)
    grad_q, grad_k_all, grad_v_all = attend_back(
        attn_probs, probs_low, query_rows, key_all, value_all, grad_attended
    )
    grad_k, grad_v = (
        lax.psum_scatter(
            grad_k_all.astype(jnp.bfloat16), "seq", scatter_dimension=1, tiled=True
        ).astype(jnp.float32),
        lax.psum_scatter(
            grad_v_all.astype(jnp.bfloat16), "seq", scatter_dimension=1, tiled=True
        ).astype(jnp.float32),
    )
    q_low = grad_q.astype(jnp.bfloat16)
    k_low = grad_k.astype(jnp.bfloat16)
    v_low = grad_v.astype(jnp.bfloat16)
    dw_query = outer_sum(normed_low, q_low)
    dw_key = outer_sum(normed_low, k_low)
    dw_value = outer_sum(normed_low, v_low)
    grad_normed = (
        project_back(q_low, back_query)
        + project_back(k_low, back_key)
        + project_back(v_low, back_value)
    )
    grad_frames_ln, dgain_attn, dbias_attn = norm_one_back(grad_normed)
    frames_grad = (grad_first + grad_frames_ln).astype(jnp.bfloat16)
    dw_query_own, dw_key_own, dw_value_own, dw_out_own, dgain_attn_own, dbias_attn_own = (
        lax.psum_scatter(dw_query, ("dp", "seq"), scatter_dimension=0, tiled=True),
        lax.psum_scatter(dw_key, ("dp", "seq"), scatter_dimension=0, tiled=True),
        lax.psum_scatter(dw_value, ("dp", "seq"), scatter_dimension=0, tiled=True),
        lax.psum_scatter(dw_out, ("dp", "seq"), scatter_dimension=0, tiled=True),
        lax.psum_scatter(dgain_attn, ("dp", "seq"), scatter_dimension=0, tiled=True),
        lax.psum_scatter(dbias_attn, ("dp", "seq"), scatter_dimension=0, tiled=True),
    )
    return (
        block_out,
        frames_grad,
        text_grad,
        dw_query_own,
        dw_key_own,
        dw_value_own,
        dw_out_own,
        dc_query_own,
        dc_key_own,
        dc_value_own,
        dc_out_own,
        dw_text_own,
        dw_up_own,
        dw_down_own,
        dgain_attn_own,
        dbias_attn_own,
        dgain_cross_own,
        dbias_cross_own,
        dgain_feed_own,
        dbias_feed_own,
    )


def solution(mesh):
    return jax.shard_map(
        on_device,
        mesh=mesh,
        in_specs=(
            P("dp", "seq", None),
            P("dp", "seq", None),
            P("dp", None, None),
            P("dp"),
            P("dp"),
            P(("dp", "seq"), None),
            P(("dp", "seq"), None),
            P(("dp", "seq"), None),
            P(("dp", "seq"), None),
            P(("dp", "seq"), None),
            P(("dp", "seq"), None),
            P(("dp", "seq"), None),
            P(("dp", "seq"), None),
            P(("dp", "seq"), None),
            P(("dp", "seq"), None),
            P(("dp", "seq"), None),
            P(("dp", "seq")),
            P(("dp", "seq")),
            P(("dp", "seq")),
            P(("dp", "seq")),
            P(("dp", "seq")),
            P(("dp", "seq")),
        ),
        out_specs=(
            P("dp", "seq", None),
            P("dp", "seq", None),
            P("dp", "seq", None),
            P(("dp", "seq"), None),
            P(("dp", "seq"), None),
            P(("dp", "seq"), None),
            P(("dp", "seq"), None),
            P(("dp", "seq"), None),
            P(("dp", "seq"), None),
            P(("dp", "seq"), None),
            P(("dp", "seq"), None),
            P(("dp", "seq"), None),
            P(("dp", "seq"), None),
            P(("dp", "seq"), None),
            P(("dp", "seq")),
            P(("dp", "seq")),
            P(("dp", "seq")),
            P(("dp", "seq")),
            P(("dp", "seq")),
            P(("dp", "seq")),
        ),
        check_vma=False,
    )
```

profile of v0, /device:TPU:0, one launch (start us, length us, event | category | flops | bytes accessed | tf_op | source)
XLA Modules:
  0.0 2470.2 jit_solution(17814668621539203134)
XLA Ops:
  16.3 42.3 %all-reduce.13 = (bf16[1024]{0:T(1024)(128)(2,1)S(1)}, bf16[1024]{0:T(1024)(128)(2,1)S(1)}, bf16[1024]{0:T(1024)(128)(2,1)S(1)}, bf16[1024]{0:T(1024)(128)(2,1)S...) all-reduce(bf16[1024]{0:T(1024)(128)(2,1)S(1)} %dynamic-update-slic, ...), channel_id=1, replica_groups=mesh['dp'=8,'seq'=4] {'dp','seq'}, use_global_device_ids=true, to_apply=%add.1 | all-reduce | flops 6144 | bytes 24576
  60.9 9.2 all-gather.20.cloned.1.call-done
  70.1 3.0 convolution_convert_fusion.8
  73.2 55.1 %all-gather.16.cloned.1.call-done = bf16[1024,1024]{1,0:T(8,128)(2,1)} async-done(((bf16[32,1024]{1,0:T(8,128)(2,1)}), bf16[1024,1024]{1,0:T(8,128)(2,1)}) %all-gather.16.cloned.1.call-update) | async-done | bytes 2097168 | tf_op jit(solution)/shard_map/all_gather | solution.py:117
  128.3 2.9 convolution_convert_fusion.10
  136.7 48.3 %all-gather.24.cloned.1.call-done = bf16[768,1024]{1,0:T(8,128)(2,1)} async-done(((bf16[24,1024]{1,0:T(8,128)(2,1)}), bf16[768,1024]{1,0:T(8,128)(2,1)}) %all-gather.24.cloned.1.call-update) | async-done | bytes 1572880 | tf_op jit(solution)/shard_map/all_gather | solution.py:123
  187.0 56.0 %all-gather.18.cloned.1.call-done = bf16[1024,1024]{1,0:T(8,128)(2,1)} async-done(((bf16[32,1024]{1,0:T(8,128)(2,1)}), bf16[1024,1024]{1,0:T(8,128)(2,1)}) %all-gather.18.cloned.1.call-update) | async-done | bytes 2097168 | tf_op jit(solution)/shard_map/all_gather | solution.py:115
  245.4 55.6 %all-gather.30.cloned.1.call-done = bf16[1024,1024]{1,0:T(8,128)(2,1)} async-done(((bf16[32,1024]{1,0:T(8,128)(2,1)}), bf16[1024,1024]{1,0:T(8,128)(2,1)}) %all-gather.30.cloned.1.call-update) | async-done | bytes 2097168 | tf_op jit(solution)/shard_map/all_gather | solution.py:120
  303.5 55.4 %all-gather.26.cloned.1.call-done = bf16[1024,1024]{1,0:T(8,128)(2,1)} async-done(((bf16[32,1024]{1,0:T(8,128)(2,1)}), bf16[1024,1024]{1,0:T(8,128)(2,1)}) %all-gather.26.cloned.1.call-update) | async-done | bytes 2097168 | tf_op jit(solution)/shard_map/all_gather | solution.py:121
  358.9 2.3 convolution_convert_fusion.1
  362.2 15.9 all-gather.40.cloned.1.call-done
  379.9 18.6 all-gather.38.cloned.1.call-done
  398.5 2.4 copy.70
  400.9 5.3 fusion.120
  406.2 4.8 fusion.26
  411.0 46.8 %all-gather.22.cloned.1.call-done = bf16[1024,1024]{1,0:T(8,128)(2,1)} async-done(((bf16[32,1024]{1,0:T(8,128)(2,1)}), bf16[1024,1024]{1,0:T(8,128)(2,1)}) %all-gather.22.cloned.1.call-update) | async-done | bytes 2097168 | tf_op jit(solution)/shard_map/all_gather | solution.py:118
  460.3 55.5 %all-gather.28.cloned.1.call-done = bf16[1024,1024]{1,0:T(8,128)(2,1)} async-done(((bf16[32,1024]{1,0:T(8,128)(2,1)}), bf16[1024,1024]{1,0:T(8,128)(2,1)}) %all-gather.28.cloned.1.call-update) | async-done | bytes 2097168 | tf_op jit(solution)/shard_map/all_gather | solution.py:119
  518.1 2.3 fusion.122
  520.5 2.4 convolution_convert_fusion.3
  522.9 51.0 %all-gather.32.cloned.1.call-done = bf16[1024,1024]{1,0:T(8,128)(2,1)} async-done(((bf16[32,1024]{1,0:T(8,128)(2,1)}), bf16[1024,1024]{1,0:T(8,128)(2,1)}) %all-gather.32.cloned.1.call-update) | async-done | bytes 2097168 | tf_op jit(solution)/shard_map/all_gather | solution.py:122
  576.4 76.6 %all-gather.34.cloned.1.call-done = bf16[1024,4096]{1,0:T(8,128)(2,1)} async-done(((bf16[32,4096]{1,0:T(8,128)(2,1)}), bf16[1024,4096]{1,0:T(8,128)(2,1)}) %all-gather.34.cloned.1.call-update) | async-done | bytes 8388624 | tf_op jit(solution)/shard_map/all_gather | solution.py:132
  652.9 11.4 multiply_convert_fusion.3
  664.3 67.5 %all-gather.36.cloned.1.call-done = bf16[4096,1024]{1,0:T(8,128)(2,1)} async-done(((bf16[128,1024]{1,0:T(8,128)(2,1)}), bf16[4096,1024]{1,0:T(8,128)(2,1)}) %all-gather.36.cloned.1.call-update) | async-done | bytes 8388624 | tf_op jit(solution)/shard_map/all_gather | solution.py:133
  731.9 8.5 add_convert_fusion
  740.4 3.1 fusion.45
  747.5 3.4 convolution_convert_fusion.2
  750.9 3.3 multiply_reduce_fusion.1
  756.7 3.7 copy.88
  762.6 3.5 fusion.46
  767.3 3.7 copy.86
  775.0 3.2 convolution_convert_fusion.5
  780.1 4.9 fusion.17
  785.1 6.4 copy.84
  791.5 3.4 copy.102
  795.0 5.2 multiply_reduce_fusion
  800.2 3.7 multiply_convert_fusion
  807.3 6.4 copy.82
  813.7 3.5 copy.103
  824.5 2.7 fusion.81
  830.4 3.9 fusion.107
  835.2 3.7 fusion.125
  839.9 2.8 fusion.67
  842.7 3.9 fusion.25
  846.7 2.8 fusion.112
  849.6 3.7 fusion.76
  854.3 3.6 fusion.79
  861.5 2.9 fusion.53
  868.8 2.8 fusion.56
  871.7 9.7 fusion.103
  882.4 9.6 fusion.70
  893.2 2.7 fusion.124
  895.9 6.3 fusion.32
  905.9 40.1 %all-reduce.12 = (f32[1024]{0:T(1024)S(1)}, f32[1024]{0:T(1024)S(1)}, f32[1024]{0:T(1024)S(1)}, f32[1024]{0:T(1024)S(1)}, f32[1024]{0:T(1024)S(1)}, /*index=5*/f32[1024]{0:T(1024)S(1)}) all-reduce(f32[1024]{0:T(1024)S(1)} %get-tuple-element.24, f32[1024]{0:T(1024)S(1)} %reduce_sum.223, ...), channel_id=19, replica_groups=mesh['dp'=8,'seq'=4] {'dp','seq'}, use_global_device_ids=true, to_apply=%region_34.35.clone | all-reduce | flops 6144 | bytes 49152
  950.4 22.5 reduce-scatter.40.cloned.1.call-done
  972.9 142.9 %reduce-scatter.32.cloned.1.call-done = f32[32,1024]{1,0:T(8,128)} async-done(((f32[1024,1024]{1,0:T(8,128)}), f32[32,1024]{1,0:T(8,128)}) %reduce-scatter.32.cloned.1.call-update) | async-done | bytes 131088 | tf_op jit(solution)/shard_map/reduce_scatter | solution.py:272
  1115.9 139.6 %reduce-scatter.38.cloned.1.call-done = f32[32,1024]{1,0:T(8,128)} async-done(((f32[1024,1024]{1,0:T(8,128)}), f32[32,1024]{1,0:T(8,128)}) %reduce-scatter.38.cloned.1.call-update) | async-done | bytes 131088 | tf_op jit(solution)/shard_map/reduce_scatter | solution.py:275
  1255.5 139.9 %reduce-scatter.30.cloned.1.call-done = f32[32,1024]{1,0:T(8,128)} async-done(((f32[1024,1024]{1,0:T(8,128)}), f32[32,1024]{1,0:T(8,128)}) %reduce-scatter.30.cloned.1.call-update) | async-done | bytes 131088 | tf_op jit(solution)/shard_map/reduce_scatter | solution.py:311
  1395.4 139.9 %reduce-scatter.24.cloned.1.call-done = f32[32,1024]{1,0:T(8,128)} async-done(((f32[1024,1024]{1,0:T(8,128)}), f32[32,1024]{1,0:T(8,128)}) %reduce-scatter.24.cloned.1.call-update) | async-done | bytes 131088 | tf_op jit(solution)/shard_map/reduce_scatter | solution.py:308
  1535.3 139.9 %reduce-scatter.36.cloned.1.call-done = f32[32,1024]{1,0:T(8,128)} async-done(((f32[1024,1024]{1,0:T(8,128)}), f32[32,1024]{1,0:T(8,128)}) %reduce-scatter.36.cloned.1.call-update) | async-done | bytes 131088 | tf_op jit(solution)/shard_map/reduce_scatter | solution.py:274
  1675.2 139.8 %reduce-scatter.34.cloned.1.call-done = f32[32,1024]{1,0:T(8,128)} async-done(((f32[1024,1024]{1,0:T(8,128)}), f32[32,1024]{1,0:T(8,128)}) %reduce-scatter.34.cloned.1.call-update) | async-done | bytes 131088 | tf_op jit(solution)/shard_map/reduce_scatter | solution.py:273
  1814.9 139.7 %reduce-scatter.28.cloned.1.call-done = f32[32,1024]{1,0:T(8,128)} async-done(((f32[1024,1024]{1,0:T(8,128)}), f32[32,1024]{1,0:T(8,128)}) %reduce-scatter.28.cloned.1.call-update) | async-done | bytes 131088 | tf_op jit(solution)/shard_map/reduce_scatter | solution.py:310
  1954.6 139.8 %reduce-scatter.26.cloned.1.call-done = f32[32,1024]{1,0:T(8,128)} async-done(((f32[1024,1024]{1,0:T(8,128)}), f32[32,1024]{1,0:T(8,128)}) %reduce-scatter.26.cloned.1.call-update) | async-done | bytes 131088 | tf_op jit(solution)/shard_map/reduce_scatter | solution.py:309
  2094.5 181.4 %reduce-scatter.42.cloned.1.call-done = f32[32,4096]{1,0:T(8,128)} async-done(((f32[1024,4096]{1,0:T(8,128)}), f32[32,4096]{1,0:T(8,128)}) %reduce-scatter.42.cloned.1.call-update) | async-done | bytes 524304 | tf_op jit(solution)/shard_map/reduce_scatter | solution.py:231
  2275.9 187.3 %reduce-scatter.44.cloned.1.call-done = f32[128,1024]{1,0:T(8,128)} async-done(((f32[4096,1024]{1,0:T(8,128)}), f32[128,1024]{1,0:T(8,128)}) %reduce-scatter.44.cloned.1.call-update) | async-done | bytes 524304 | tf_op jit(solution)/shard_map/reduce_scatter | solution.py:232
  (226 shorter events, 83.1 us)
Async XLA Ops:
  7.2 177.8 %copy-start = (bf16[1,256,768]{2,1,0:T(8,128)(2,1)S(1)}, bf16[1,256,768]{2,1,0:T(8,128)(2,1)}, u32[]{:S(2)}) copy-start(bf16[1,256,768]{2,1,0:T(8,128)(2,1)} %param.24) | copy-start | bytes 1179652
  7.2 121.1 %copy-start.1 = (bf16[1,160,1024]{2,1,0:T(8,128)(2,1)S(1)}, bf16[1,160,1024]{2,1,0:T(8,128)(2,1)}, u32[]{:S(2)}) copy-start(bf16[1,160,1024]{2,1,0:T(8,128)(2,1)} %param.22) | copy-start | bytes 983044
  7.2 62.9 %all-gather.20.cloned.1.call-start = ((), (), s32[]{:S(2)}) async-start(), calls=%async_computation.17 | async-start | bytes 2162688 | tf_op jit(solution)/shard_map/all_gather | solution.py:116
  7.9 120.3 %all-gather.16.cloned.1.call-start = ((), (), s32[]{:S(2)}) async-start(), calls=%async_computation.15 | async-start | bytes 2162688 | tf_op jit(solution)/shard_map/all_gather | solution.py:117
  8.7 176.3 %all-gather.24.cloned.1.call-start = ((), (), s32[]{:S(2)}) async-start(), calls=%async_computation.19 | async-start | bytes 1622016 | tf_op jit(solution)/shard_map/all_gather | solution.py:123
  9.4 233.6 %all-gather.18.cloned.1.call-start = ((), (), s32[]{:S(2)}) async-start(), calls=%async_computation.16 | async-start | bytes 2162688 | tf_op jit(solution)/shard_map/all_gather | solution.py:115
  10.0 291.0 %all-gather.30.cloned.1.call-start = ((), (), s32[]{:S(2)}) async-start(), calls=%async_computation.22 | async-start | bytes 2162688 | tf_op jit(solution)/shard_map/all_gather | solution.py:120
  10.6 348.3 %all-gather.26.cloned.1.call-start = ((), (), s32[]{:S(2)}) async-start(), calls=%async_computation.20 | async-start | bytes 2162688 | tf_op jit(solution)/shard_map/all_gather | solution.py:121
  11.2 367.0 %all-gather.40.cloned.1.call-start = ((), (), s32[]{:S(2)}) async-start(), calls=%async_computation.38 | async-start | bytes 1638400 | tf_op jit(solution)/shard_map/all_gather | solution.py:166
  60.9 70.3 %copy-start.38 = (f32[160]{0:T(256)}, f32[160]{0:T(256)S(1)}, u32[]{:S(2)}) copy-start(f32[160]{0:T(256)S(1)} %fusion.43) | copy-start | bytes 1924
  73.1 325.4 %all-gather.38.cloned.1.call-start = ((), (), s32[]{:S(2)}) async-start(), calls=%async_computation.37 | async-start | bytes 1638400 | tf_op jit(solution)/shard_map/all_gather | solution.py:167
  131.2 326.6 %all-gather.22.cloned.1.call-start = ((), (), s32[]{:S(2)}) async-start(), calls=%async_computation.18 | async-start | bytes 2162688 | tf_op jit(solution)/shard_map/all_gather | solution.py:118
  131.9 383.8 %all-gather.28.cloned.1.call-start = ((), (), s32[]{:S(2)}) async-start(), calls=%async_computation.21 | async-start | bytes 2162688 | tf_op jit(solution)/shard_map/all_gather | solution.py:119
  132.5 441.3 %all-gather.32.cloned.1.call-start = ((), (), s32[]{:S(2)}) async-start(), calls=%async_computation.23 | async-start | bytes 2162688 | tf_op jit(solution)/shard_map/all_gather | solution.py:122
  133.3 519.7 %all-gather.34.cloned.1.call-start = ((), (), s32[]{:S(2)}) async-start(), calls=%async_computation.24 | async-start | bytes 8650752 | tf_op jit(solution)/shard_map/all_gather | solution.py:132
  133.8 598.0 %all-gather.36.cloned.1.call-start = ((), (), s32[]{:S(2)}) async-start(), calls=%async_computation.25 | async-start | bytes 8650752 | tf_op jit(solution)/shard_map/all_gather | solution.py:133
  134.6 682.8 %reduce-scatter.52.cloned.1.call-start = ((), (), s32[]{:S(2)}) async-start(), calls=%async_computation.42 | async-start | bytes 655360
  187.0 172.0 %copy-start.36 = (bf16[256,1024]{1,0:T(8,128)(2,1)}, bf16[256,1024]{1,0:T(8,128)(2,1)S(1)}, u32[]{:S(2)}) copy-start(bf16[256,1024]{1,0:T(8,128)(2,1)S(1)} %convolution_convert_fusion.4) | copy-start | bytes 1572868
  245.4 155.6 %copy-start.25 = (bf16[160,1024]{0,1:T(8,128)(2,1)}, bf16[160,1024]{0,1:T(8,128)(2,1)S(1)}, u32[]{:S(2)}) copy-start(bf16[160,1024]{0,1:T(8,128)(2,1)S(1)} %copy.90) | copy-start | bytes 983044
  303.5 444.0 %copy-start.30 = (bf16[256,1024]{0,1:T(8,128)(2,1)}, bf16[256,1024]{0,1:T(8,128)(2,1)S(1)}, u32[]{:S(2)}) copy-start(bf16[256,1024]{0,1:T(8,128)(2,1)S(1)} %copy.74) | copy-start | bytes 1572868
  379.9 26.4 %copy-start.11 = (bf16[640,1024]{0,1:T(8,128)(2,1)}, bf16[640,1024]{0,1:T(8,128)(2,1)S(1)}, u32[]{:S(2)}) copy-start(bf16[640,1024]{0,1:T(8,128)(2,1)S(1)} %copy.71) | copy-start | bytes 3932164
  411.0 106.9 %copy-start.32 = (bf16[16,64,160]{2,1,0:T(8,128)(2,1)}, bf16[16,64,160]{2,1,0:T(8,128)(2,1)S(1)}, u32[]{:S(2)}) copy-start(bf16[16,64,160]{2,1,0:T(8,128)(2,1)S(1)} %fusion.26) | copy-start | bytes 983044
  518.1 4.7 copy-start.34
  522.9 53.5 %copy-start.24 = (bf16[16,64,160]{2,1,0:T(8,128)(2,1)}, bf16[16,64,160]{2,1,0:T(8,128)(2,1)S(1)}, u32[]{:S(2)}) copy-start(bf16[16,64,160]{2,1,0:T(8,128)(2,1)S(1)} %convolution_convert_fusion.3) | copy-start | bytes 983044
  576.4 155.5 %copy-start.19 = (bf16[1,160,1024]{2,1,0:T(8,128)(2,1)S(1)}, bf16[1,160,1024]{2,1,0:T(8,128)(2,1)}, u32[]{:S(2)}) copy-start(bf16[1,160,1024]{2,1,0:T(8,128)(2,1)} %param.23) | copy-start | bytes 983044
  731.9 8.5 copy-start.4
  740.4 3.1 copy-start.10
  743.5 1.4 copy-start.8
  743.5 2.1 copy-start.3
  747.5 3.4 copy-start.37
  750.9 3.3 copy-start.21
  754.2 1.1 copy-start.31
  762.6 58.4 %reduce-scatter.50.cloned.1.call-start = ((), (), s32[]{:S(2)}) async-start(), calls=%async_computation.41 | async-start | bytes 655360
  762.6 3.6 copy-start.35
  767.3 5.9 copy-start.6
  774.9 83.0 %reduce-scatter.48.cloned.1.call-start = ((), (), s32[]{:S(2)}) async-start(), calls=%async_computation.40 | async-start | bytes 1638400
  794.9 70.4 %reduce-scatter.46.cloned.1.call-start = ((), (), s32[]{:S(2)}) async-start(), calls=%async_computation.39 | async-start | bytes 1638400
  800.2 5.4 copy-start.26
  803.9 1.7 copy-start.2
  817.3 155.7 %reduce-scatter.40.cloned.1.call-start = ((), (), s32[]{:S(2)}) async-start(), calls=%async_computation.34 | async-start | bytes 3244032 | tf_op jit(solution)/shard_map/reduce_scatter | solution.py:276
  824.5 2.7 copy-start.23
  824.5 2.8 copy-start.28
  830.3 285.6 %reduce-scatter.32.cloned.1.call-start = ((), (), s32[]{:S(2)}) async-start(), calls=%async_computation.30 | async-start | bytes 4325376 | tf_op jit(solution)/shard_map/reduce_scatter | solution.py:272
  834.2 421.3 %reduce-scatter.38.cloned.1.call-start = ((), (), s32[]{:S(2)}) async-start(), calls=%async_computation.33 | async-start | bytes 4325376 | tf_op jit(solution)/shard_map/reduce_scatter | solution.py:275
  838.9 1.0 copy-start.33
  838.9 556.5 %reduce-scatter.30.cloned.1.call-start = ((), (), s32[]{:S(2)}) async-start(), calls=%async_computation.29 | async-start | bytes 4325376 | tf_op jit(solution)/shard_map/reduce_scatter | solution.py:311
  842.7 692.6 %reduce-scatter.24.cloned.1.call-start = ((), (), s32[]{:S(2)}) async-start(), calls=%async_computation.26 | async-start | bytes 4325376 | tf_op jit(solution)/shard_map/reduce_scatter | solution.py:308
  846.7 2.9 copy-start.12
  849.5 825.7 %reduce-scatter.36.cloned.1.call-start = ((), (), s32[]{:S(2)}) async-start(), calls=%async_computation.32 | async-start | bytes 4325376 | tf_op jit(solution)/shard_map/reduce_scatter | solution.py:274
  853.3 961.6 %reduce-scatter.34.cloned.1.call-start = ((), (), s32[]{:S(2)}) async-start(), calls=%async_computation.31 | async-start | bytes 4325376 | tf_op jit(solution)/shard_map/reduce_scatter | solution.py:273
  857.9 1096.7 %reduce-scatter.28.cloned.1.call-start = ((), (), s32[]{:S(2)}) async-start(), calls=%async_computation.28 | async-start | bytes 4325376 | tf_op jit(solution)/shard_map/reduce_scatter | solution.py:310
  861.5 2.9 copy-start.13
  864.4 1230.1 %reduce-scatter.26.cloned.1.call-start = ((), (), s32[]{:S(2)}) async-start(), calls=%async_computation.27 | async-start | bytes 4325376 | tf_op jit(solution)/shard_map/reduce_scatter | solution.py:309
  868.8 2.9 copy-start.15
  871.7 1404.2 %reduce-scatter.42.cloned.1.call-start = ((), (), s32[]{:S(2)}) async-start(), calls=%async_computation.35 | async-start | bytes 17301504 | tf_op jit(solution)/shard_map/reduce_scatter | solution.py:231
  881.4 1.0 copy-start.20
  881.4 1581.8 %reduce-scatter.44.cloned.1.call-start = ((), (), s32[]{:S(2)}) async-start(), calls=%async_computation.36 | async-start | bytes 17301504 | tf_op jit(solution)/shard_map/reduce_scatter | solution.py:232
  892.0 1.1 copy-start.9
  895.8 6.4 copy-start.5
  895.8 7.7 copy-start.16
  895.8 7.7 copy-start.29
  902.2 2.2 copy-start.14
  902.2 2.2 copy-start.27
  904.4 1.1 copy-start.39
  (4 other events, 3.5 us)
Sparse Core Ops, SparseCore 0:
  10.9 59.1 all-gather.19
  72.9 55.3 all-gather.15
  131.2 53.7 all-gather.23
  187.7 55.2 all-gather.17
  245.7 55.2 all-gather.29
  303.7 55.2 all-gather.25
  361.1 17.0 all-gather.39
  380.3 18.1 all-gather.37
  401.4 56.3 all-gather.21
  460.5 55.2 all-gather.27
  518.6 55.2 all-gather.31
  576.6 76.2 all-gather.33
  655.8 76.0 all-gather.35
  762.7 20.2 reduce-scatter.51
  785.4 21.6 reduce-scatter.49
  809.5 26.5 reduce-scatter.47
  838.6 26.6 reduce-scatter.45
  871.1 101.7 reduce-scatter.39
  975.8 140.0 reduce-scatter.31
  1118.6 136.9 reduce-scatter.37
  1258.4 136.9 reduce-scatter.29
  1398.2 137.0 reduce-scatter.23
  1538.2 136.9 reduce-scatter.35
  1677.9 137.0 reduce-scatter.33
  1817.8 136.7 reduce-scatter.27
  1957.3 137.0 reduce-scatter.25
  2097.2 178.6 reduce-scatter.41
  2278.7 184.4 reduce-scatter.43
where the time goes:
time: 2480 us; the launch traced here: 2470 us
  waiting for transfers between devices  2130 us (86%)
  matrix products  155 us (6%)
  blocking collectives  82.4 us (3%)
  local copies, waits for them, and re-layouts  70.3 us (3%)
    reduce_scatter x1, waiting for transfers between devices, on_device(): lax.psum_scatter(dw_down, ('dp', 'seq'), scatter_dimension=0, tiled=True)  187 us
    reduce_scatter x1, waiting for transfers between devices, on_device(): lax.psum_scatter(dw_up, ('dp', 'seq'), scatter_dimension=0, tiled=True)  181 us
    reduce_scatter x1, waiting for transfers between devices, on_device(): lax.psum_scatter(dc_query, ('dp', 'seq'), scatter_dimension=0, tiled=True)  143 us
    reduce_scatter x1, waiting for transfers between devices, on_device(): lax.psum_scatter(dw_query, ('dp', 'seq'), scatter_dimension=0, tiled=True)  140 us
    reduce_scatter x1, waiting for transfers between devices, on_device(): lax.psum_scatter(dc_value, ('dp', 'seq'), scatter_dimension=0, tiled=True)  140 us
    reduce_scatter x1, waiting for transfers between devices, on_device(): lax.psum_scatter(dw_out, ('dp', 'seq'), scatter_dimension=0, tiled=True)  140 us
    reduce_scatter x1, waiting for transfers between devices, on_device(): lax.psum_scatter(dw_key, ('dp', 'seq'), scatter_dimension=0, tiled=True)  140 us
    reduce_scatter x1, waiting for transfers between devices, on_device(): lax.psum_scatter(dc_key, ('dp', 'seq'), scatter_dimension=0, tiled=True)  140 us
  transfers between devices with their start and end apart: 28, of which 25 were waited for; matrix products, arithmetic and copies ran while one was open for 8% of the time, Pallas kernels for 0%

commit v1 on v0

v1 whole, which is shorter than its diff:
```python
import functools
from typing import NamedTuple
import jax
import jax.numpy as jnp
from jax import lax
from jax.experimental import pallas as pl
from jax.experimental.pallas import tpu as pltpu
from jax.sharding import PartitionSpec as P

MESH = pl.DeviceIdType.MESH

LAG = 2
VMEM_LIMIT = 60 * 1024 * 1024

def unit_ops(perm, nz):
    rank = {a: i for i, a in enumerate(perm)}
    ops = {}

    def source(j, fy, fx):
        differs = [a for a, f in (("z", j > 0), ("y", fy), ("x", fx)) if f]
        if not differs:
            return None
        last = max(differs, key=lambda a: rank[a])
        if last == "z":
            return ("z", j - 1, fy, fx)
        if last == "y":
            return ("y", j, 0, fx)
        return ("x", j, fy, 0)

    for j in range(nz):
        for fy in range(2):
            for fx in range(2):
                for axis in "zyx":
                    flags = {"z": j > 0, "y": fy, "x": fx}
                    if axis != "z" and flags[axis]:
                        continue
                    if any(flags[a] and rank[a] > rank[axis] for a in "zyx" if a != axis):
                        continue
                    if axis == "z" and j == nz - 1:
                        continue
                    ops[(axis, j, fy, fx)] = source(j, fy, fx)
    return ops

def make_schedule(perms, nz, lag=LAG, window=None):
    ops = {}
    for u, perm in enumerate(perms):
        for key, dep in unit_ops(perm, nz).items():
            ops[(u,) + key] = None if dep is None else (u,) + dep
    children = {}
    for op, dep in ops.items():
        children.setdefault(dep, []).append(op)
    height = {}

    def tall(op):
        if op not in height:
            height[op] = 1 + max([tall(c) for c in children.get(op, [])], default=0)
        return height[op]

    for op in ops:
        tall(op)
    done, slots, left = {}, [], set(ops)
    while left:
        t = len(slots)
        slot = {}
        for axis in "zyx":
            ready = [op for op in left if op[1] == axis and (ops[op] is None or (ops[op] in done and done[ops[op]] + lag <= t))]
            if ready:
                slot[axis] = min(ready, key=lambda op: (op[0] // window if window else 0, -height[op], op[0], op))
        for axis, op in slot.items():
            done[op] = t
            left.discard(op)
        slots.append(slot)
    return slots

def nth_table(nz):
    rows = []
    for z in range(nz):
        offs = sorted((p - z for p in range(nz)), key=lambda o: (abs(o), o if z % 2 else -o))
        rows.append([z + o for o in offs])
    return rows

def pick(values, z):
    out = 0
    for i, v in enumerate(values):
        out = out + v * jnp.where(z == i, 1, 0)
    return out

UP, DOWN, YY, XX, CORE = range(5)
WAYS_OF = dict(z=(UP, DOWN), y=(YY,), x=(XX,))

class Place:
    def __init__(self, nz):
        d, s = lax.axis_index("dp"), lax.axis_index("seq")
        self.nz = nz
        self.z, self.y, self.x, self.c = d // 2, d % 2, s // 2, s % 2
        z, y, x, c = self.z, self.y, self.x, self.c
        self.device = [
            ((z + 1) * 2 + y, x * 2 + c),
            ((z - 1) * 2 + y, x * 2 + c),
            (z * 2 + 1 - y, x * 2 + c),
            (z * 2 + y, (1 - x) * 2 + c),
            (z * 2 + y, x * 2 + 1 - c),
        ]
        self.nth = [[row[j] for row in nth_table(nz)] for j in range(nz)]

    def greet(self):
        barrier = pltpu.get_barrier_semaphore()
        has_up, has_down = self.z + 1 < self.nz, self.z > 0
        for way in range(5):
            def hello(way=way):
                pl.semaphore_signal(barrier, inc=1, device_id=self.device[way], device_id_type=MESH)
            if way < YY:
                pl.when(has_up if way == UP else has_down)(hello)
            else:
                hello()
        edge = jnp.where(self.z == 0, 1, 0) + jnp.where(self.z == self.nz - 1, 1, 0)
        pl.semaphore_wait(barrier, 5 - edge)

    def gather_moves(self, axis, j, fy, fx):
        z, y, x, nz = self.z, self.y, self.x, self.nz
        py, px = (1 - y if fy else y), (1 - x if fx else x)
        if axis == "z":
            out = [(UP, (z - j >= 0) & (z + 1 < nz), (z - j, py, px)), (DOWN, (z + j < nz) & (z > 0), (z + j, py, px))]
            come = [(UP, z - 1 - j >= 0, (z - 1 - j, py, px)), (DOWN, z + 1 + j < nz, (z + 1 + j, py, px))]
        else:
            pz = pick(self.nth[j], z)
            there = (pz, 1 - y, px) if axis == "y" else (pz, py, 1 - x)
            way = YY if axis == "y" else XX
            out = [(way, None, (pz, py, px))]
            come = [(way, None, there)]
        return out, come

def when(cond, fn):
    if cond is None:
        fn()
    else:
        pl.when(cond)(fn)

def gather_body(nz, units, slots, n, depth, *refs):
    given, outs, rows_out = refs[:n + 1], refs[n + 1:2 * n + 1], refs[2 * n + 1]
    held = refs[2 * n + 2:3 * n + 3]
    ins, rows_in = held[:n], held[n]
    send_sem, recv_sem, core_send, core_recv, local_sem, rows_send, rows_recv = refs[3 * n + 3:]
    loads = [pltpu.make_async_copy(given[g], held[g], local_sem.at[g]) for g in range(n + 1)]
    for cp in loads:
        cp.start()
    here = Place(nz)
    z, y, x, c = here.z, here.y, here.x, here.c
    own = [pltpu.make_async_copy(ins[g], outs[g].at[z, y, x, c], local_sem.at[g]) for g in range(n)]
    own.append(pltpu.make_async_copy(rows_in, rows_out.at[x, c], local_sem.at[n]))
    here.greet()
    for cp in loads:
        cp.wait()
    for cp in own:
        cp.start()

    def rows_over(src, dst, way, i):
        return pltpu.make_async_remote_copy(
            src_ref=src, dst_ref=dst, send_sem=rows_send.at[i], recv_sem=rows_recv.at[i],
            device_id=here.device[way], device_id_type=MESH,
        )

    rows_moves = [
        rows_over(rows_in, rows_out.at[x, c], XX, 0),
        rows_over(rows_in, rows_out.at[x, c], CORE, 1),
        rows_over(rows_out.at[1 - x, c], rows_out.at[1 - x, c], CORE, 2),
    ]
    rows_moves[0].start()
    rows_moves[1].start()

    def piece(u, p):
        g, r0, rn, c0, cn = units[u]
        return outs[g].at[p[0], p[1], p[2], c, pl.ds(r0, rn), pl.ds(c0, cn)]

    def corner(u, fy, fx, which):
        g, r0, rn, c0, cn = units[u]
        return outs[g].at[:, 1 - y if fy else y, 1 - x if fx else x, which, pl.ds(r0, rn), pl.ds(c0, cn)]

    def remote(u, way, t, p, mine):
        i = way
        ref = piece(u, p)
        g, r0, rn, c0, cn = units[u]
        src = ins[g].at[pl.ds(r0, rn), pl.ds(c0, cn)] if mine else ref
        return pltpu.make_async_remote_copy(src_ref=src, dst_ref=ref, send_sem=send_sem.at[i, t], recv_sem=recv_sem.at[i, t], device_id=here.device[way], device_id_type=MESH)

    def across(u, fy, fx):
        ref = corner(u, fy, fx, c)
        i = fy * 2 + fx
        return pltpu.make_async_remote_copy(src_ref=ref, dst_ref=ref, send_sem=core_send.at[u, i], recv_sem=core_recv.at[u, i], device_id=here.device[CORE], device_id_type=MESH)

    last = {}
    for t, slot in enumerate(slots):
        for u, axis, j, fy, fx in slot.values():
            came = {"z": (u, fy, fx), "y": (u, 1, fx), "x": (u, fy, 1)}[axis]
            last[came] = t
    for t in range(len(slots) + depth):
        if t < len(slots):
            for axis, (u, _, j, fy, fx) in slots[t].items():
                for way, cond, p in here.gather_moves(axis, j, fy, fx)[0]:
                    when(cond, lambda u=u, way=way, p=p: remote(u, way, t, p, (j, fy, fx) == (0, 0, 0)).start())
        if t == depth - 1:
            for cp in own:
                cp.wait()
        if t == min(6, len(slots) - 1):
            arrived = rows_out.at[1 - x, c]
            pltpu.make_async_copy(arrived, arrived, rows_recv.at[0]).wait()
            rows_moves[2].start()
        if t >= depth:
            for axis, (u, _, j, fy, fx) in slots[t - depth].items():
                for way, cond, p in here.gather_moves(axis, j, fy, fx)[1]:
                    when(cond, lambda u=u, way=way, p=p: pltpu.make_async_copy(piece(u, p), piece(u, p), recv_sem.at[way, t - depth]).wait())
            for key in sorted(last):
                if last[key] == t - depth:
                    across(*key).start()
    for t, slot in enumerate(slots):
        for axis, (u, _, j, fy, fx) in slot.items():
            for way, cond, p in here.gather_moves(axis, j, fy, fx)[0]:
                when(cond, lambda u=u, way=way, p=p: remote(u, way, t, p, (j, fy, fx) == (0, 0, 0)).wait_send())
    for u, fy, fx in sorted(last):
        across(u, fy, fx).wait_send()
    for u, fy, fx in sorted(last):
        ref = corner(u, fy, fx, 1 - c)
        pltpu.make_async_copy(ref, ref, core_recv.at[u, fy * 2 + fx]).wait()
    for cp in rows_moves:
        cp.wait_send()
    for i, ref in ((1, rows_out.at[x, 1 - c]), (2, rows_out.at[1 - x, 1 - c])):
        pltpu.make_async_copy(ref, ref, rows_recv.at[i]).wait()

def gather_weights(arrays, frame_rows, units, perms, nz, window=None, depth=2):
    n = len(arrays)
    slots = make_schedule(perms, nz, lag=depth + 1, window=window)
    return pl.pallas_call(
        functools.partial(gather_body, nz, units, slots, n, depth),
        out_shape=[jax.ShapeDtypeStruct((nz, 2, 2, 2) + a.shape, a.dtype) for a in arrays]
        + [jax.ShapeDtypeStruct((2, 2) + frame_rows.shape, frame_rows.dtype)],
        in_specs=[pl.BlockSpec(memory_space=pl.ANY)] * (n + 1),
        out_specs=[pl.BlockSpec(memory_space=pl.ANY)] * (n + 1),
        scratch_shapes=[pltpu.VMEM(a.shape, a.dtype) for a in (*arrays, frame_rows)]
        + [
            pltpu.SemaphoreType.DMA((4, len(slots))),
            pltpu.SemaphoreType.DMA((4, len(slots))),
            pltpu.SemaphoreType.DMA((len(units), 4)),
            pltpu.SemaphoreType.DMA((len(units), 4)),
            pltpu.SemaphoreType.DMA((n + 1,)),
            pltpu.SemaphoreType.DMA((3,)),
            pltpu.SemaphoreType.DMA((3,)),
        ],
        compiler_params=pltpu.CompilerParams(collective_id=1, has_side_effects=True, vmem_limit_bytes=16 * 1024 * 1024),
        name="gather_weights",
    )(*arrays, frame_rows)


BACK = (DOWN, UP, YY, XX)


def scatter_body(nz, units, slots, n, depth, *refs):
    ins, out = refs[:n], refs[n]
    total, twin, landed, send_sem, recv_sem, core_send, core_recv, local_sem = refs[n + 1:]
    here = Place(nz)
    z, y, x, c = here.z, here.y, here.x, here.c
    steps = slots[::-1]
    numbers, order = {}, []
    for t, slot in enumerate(steps):
        for axis, op in slot.items():
            for way in WAYS_OF[axis]:
                numbers[way, t] = len(numbers)
            if op[0] not in order:
                order.append(op[0])

    def plane(u, which):
        g, r0, rn, c0, cn = units[u]
        return ins[g].at[:, :, :, which, pl.ds(r0, rn), pl.ds(c0, cn)]

    def local(u):
        return pltpu.make_async_copy(plane(u, c), total.at[u], local_sem.at[u])

    def across(u):
        return pltpu.make_async_remote_copy(
            src_ref=plane(u, 1 - c), dst_ref=twin.at[u], send_sem=core_send.at[u], recv_sem=core_recv.at[u],
            device_id=here.device[CORE], device_id_type=MESH,
        )

    def remote(u, way, t, p):
        i = numbers[way, t]
        return pltpu.make_async_remote_copy(
            src_ref=total.at[u, p[0], p[1], p[2]], dst_ref=landed.at[i], send_sem=send_sem.at[i], recv_sem=recv_sem.at[i],
            device_id=here.device[BACK[way]], device_id_type=MESH,
        )

    for u in order:
        local(u).start()
    here.greet()
    for u in order:
        across(u).start()

    def join(u):
        local(u).wait()
        across(u).wait_recv()

        @pl.loop(0, nz)
        def _(a):
            for b in range(2):
                for e in range(2):
                    total[u, a, b, e] = (
                        total[u, a, b, e].astype(jnp.float32) + twin[u, a, b, e].astype(jnp.float32)
                    ).astype(jnp.bfloat16)

    joined = set()
    for t in range(len(steps) + depth):
        if t < len(steps):
            for axis, (u, _, j, fy, fx) in steps[t].items():
                if u not in joined:
                    joined.add(u)
                    join(u)
                for way, cond, p in here.gather_moves(axis, j, fy, fx)[1]:
                    when(cond, lambda u=u, way=way, p=p: remote(u, way, t, p).start())
        if t >= depth:
            s = t - depth
            for axis, (u, _, j, fy, fx) in steps[s].items():
                for way, cond, p in here.gather_moves(axis, j, fy, fx)[0]:
                    def add(u=u, way=way, p=p):
                        i = numbers[way, s]
                        pltpu.make_async_copy(landed.at[i], landed.at[i], recv_sem.at[i]).wait()
                        total[u, p[0], p[1], p[2]] = (
                            total[u, p[0], p[1], p[2]].astype(jnp.float32) + landed[i].astype(jnp.float32)
                        ).astype(jnp.bfloat16)
                    when(cond, add)
    for u in range(len(units)):
        out[u] = total[u, z, y, x].astype(jnp.float32)
    for t, slot in enumerate(steps):
        for axis, (u, _, j, fy, fx) in slot.items():
            for way, cond, p in here.gather_moves(axis, j, fy, fx)[1]:
                when(cond, lambda u=u, way=way, p=p: remote(u, way, t, p).wait_send())
    for u in order:
        across(u).wait_send()


def scatter_grads(arrays, units, perms, nz, depth=2):
    n = len(arrays)
    slots = make_schedule(perms, nz, lag=depth + 1)
    count = sum(2 if axis == "z" else 1 for slot in slots for axis in slot)
    rows, columns = units[0][2], units[0][4]
    return pl.pallas_call(
        functools.partial(scatter_body, nz, units, slots, n, depth),
        out_shape=jax.ShapeDtypeStruct((len(units), rows, columns), jnp.float32),
        in_specs=[pl.BlockSpec(memory_space=pl.ANY)] * n,
        out_specs=pl.BlockSpec(memory_space=pltpu.VMEM),
        scratch_shapes=[
            pltpu.VMEM((len(units), nz, 2, 2, rows, columns), jnp.bfloat16),
            pltpu.VMEM((len(units), nz, 2, 2, rows, columns), jnp.bfloat16),
            pltpu.VMEM((count, rows, columns), jnp.bfloat16),
            pltpu.SemaphoreType.DMA((count,)),
            pltpu.SemaphoreType.DMA((count,)),
            pltpu.SemaphoreType.DMA((len(units),)),
            pltpu.SemaphoreType.DMA((len(units),)),
            pltpu.SemaphoreType.DMA((len(units),)),
        ],
        compiler_params=pltpu.CompilerParams(collective_id=2, has_side_effects=True, vmem_limit_bytes=VMEM_LIMIT),
        name="scatter_grads",
    )(*arrays)


def share_body(n, chunk, *refs):
    ins, outs = refs[:n], refs[n:2 * n]
    twins, sums, landed = refs[2 * n:3 * n], refs[3 * n:4 * n], refs[4 * n:5 * n]
    core_send, core_recv, x_send, x_recv = refs[5 * n:]
    d, s = lax.axis_index("dp"), lax.axis_index("seq")
    x, c = s // 2, s % 2
    core, over = (d, x * 2 + 1 - c), (d, (1 - x) * 2 + c)
    barrier = pltpu.get_barrier_semaphore()
    for other in (core, over):
        pl.semaphore_signal(barrier, inc=1, device_id=other, device_id_type=MESH)
    pl.semaphore_wait(barrier, 2)
    pieces = [(g, k, pl.ds(k * chunk, chunk)) for g in range(n) for k in range(ins[g].shape[2] // chunk)]

    def across(i, far):
        g, k, rows = pieces[i]
        part = 1 - x if far else x
        return pltpu.make_async_remote_copy(
            src_ref=ins[g].at[part, 1 - c, rows], dst_ref=twins[g].at[1 if far else 0, rows],
            send_sem=core_send.at[1 if far else 0, i], recv_sem=core_recv.at[1 if far else 0, i],
            device_id=core, device_id_type=MESH,
        )

    def beyond(i):
        g, k, rows = pieces[i]
        return pltpu.make_async_remote_copy(
            src_ref=sums[g].at[rows], dst_ref=landed[g].at[rows], send_sem=x_send.at[i], recv_sem=x_recv.at[i],
            device_id=over, device_id_type=MESH,
        )

    for far in (True, False):
        for i in range(len(pieces)):
            across(i, far).start()
    for i, (g, k, rows) in enumerate(pieces):
        across(i, True).wait_recv()
        sums[g][rows] = (ins[g][1 - x, c, rows].astype(jnp.float32) + twins[g][1, rows].astype(jnp.float32)).astype(jnp.bfloat16)
        beyond(i).start()
    for i, (g, k, rows) in enumerate(pieces):
        across(i, False).wait_recv()
        beyond(i).wait_recv()
        outs[g][rows] = (
            ins[g][x, c, rows].astype(jnp.float32) + twins[g][0, rows].astype(jnp.float32) + landed[g][rows].astype(jnp.float32)
        ).astype(jnp.bfloat16)
    for i in range(len(pieces)):
        across(i, True).wait_send()
        across(i, False).wait_send()
        beyond(i).wait_send()


def share_sums(arrays, number):
    n = len(arrays)
    chunk = 32
    count = sum(a.shape[2] // chunk for a in arrays)
    return pl.pallas_call(
        functools.partial(share_body, n, chunk),
        out_shape=[jax.ShapeDtypeStruct(a.shape[2:], a.dtype) for a in arrays],
        in_specs=[pl.BlockSpec(memory_space=pltpu.VMEM)] * n,
        out_specs=[pl.BlockSpec(memory_space=pltpu.VMEM)] * n,
        scratch_shapes=[pltpu.VMEM((2,) + a.shape[2:], a.dtype) for a in arrays]
        + [pltpu.VMEM(a.shape[2:], a.dtype) for a in arrays] * 2
        + [pltpu.SemaphoreType.DMA((2, count))] * 2
        + [pltpu.SemaphoreType.DMA((count,))] * 2,
        compiler_params=pltpu.CompilerParams(collective_id=number, has_side_effects=True, vmem_limit_bytes=32 * 1024 * 1024),
        name="share_sums",
    )(*arrays)


def deliver_body(units, text_rows, sums, *outs):
    for u, (g, r0, rn, c0, cn) in enumerate(units):
        if g == 8:
            outs[g][...] = sums[u, :text_rows]
            outs[-1][...] = sums[u, text_rows:text_rows + 8]
        else:
            outs[g][r0:r0 + rn, c0:c0 + cn] = sums[u]


def deliver(sums, units, text_rows, shapes):
    shapes = [(text_rows,) + s[1:] if g == 8 else s for g, s in enumerate(shapes)] + [(8, sums.shape[2])]
    return pl.pallas_call(
        functools.partial(deliver_body, units, text_rows),
        out_shape=[jax.ShapeDtypeStruct(s, sums.dtype) for s in shapes],
        compiler_params=pltpu.CompilerParams(vmem_limit_bytes=16 * 1024 * 1024),
        name="deliver",
    )(sums)


def pair_scores(bounds_ref, q, k, keep, causal):
    s = lax.dot_general(jnp.where(keep, q, 0), k, (((1,), (1,)), ((), ())), preferred_element_type=jnp.float32)
    col = lax.broadcasted_iota(jnp.int32, s.shape, 1)
    if causal:
        row = lax.broadcasted_iota(jnp.int32, s.shape, 0) + bounds_ref[0]
        seen = (col <= row) & ((col >= bounds_ref[1]) | (col == row))
    else:
        seen = col < bounds_ref[0]
    s = jnp.where(seen, s * 0.125, -1e30)
    e = jnp.exp(s - jnp.max(s, axis=1, keepdims=True))
    return e * (1.0 / jnp.sum(e, axis=1, keepdims=True))


def halves(width):
    lane = lax.broadcasted_iota(jnp.int32, (1, width), 1)
    return [(lane >= 64 * h) & (lane < 64 * h + 64) for h in range(width // 64)]


def attend_body(causal, bounds_ref, q_ref, k_ref, v_ref, out_ref):
    q, k, v = q_ref[...], k_ref[...], v_ref[...]
    out = None
    for keep in halves(q.shape[1]):
        p = pair_scores(bounds_ref, q, k, keep, causal)
        o = jnp.dot(p.astype(jnp.bfloat16), v, preferred_element_type=jnp.float32)
        out = o if out is None else jnp.where(keep, o, out)
    out_ref[...] = out.astype(jnp.bfloat16)


def attend_back_body(causal, bounds_ref, q_ref, k_ref, v_ref, g_ref, dq_ref, dk_ref, dv_ref):
    q, k, v, g = q_ref[...], k_ref[...], v_ref[...], g_ref[...]
    dq = dk = dv = None
    for keep in halves(q.shape[1]):
        p = pair_scores(bounds_ref, q, k, keep, causal)
        dp = lax.dot_general(jnp.where(keep, g, 0), v, (((1,), (1,)), ((), ())), preferred_element_type=jnp.float32)
        ds = (p * (dp - jnp.sum(p * dp, axis=1, keepdims=True))).astype(jnp.bfloat16)
        a = jnp.dot(ds, k, preferred_element_type=jnp.float32)
        b = lax.dot_general(ds, q, (((0,), (0,)), ((), ())), preferred_element_type=jnp.float32)
        e = lax.dot_general(p.astype(jnp.bfloat16), g, (((0,), (0,)), ((), ())), preferred_element_type=jnp.float32)
        if dq is None:
            dq, dk, dv = a, b, e
        else:
            dq, dk, dv = jnp.where(keep, a, dq), jnp.where(keep, b, dk), jnp.where(keep, e, dv)
    dq_ref[...] = (dq * 0.125).astype(jnp.bfloat16)
    dk_ref[...] = (dk * 0.125).astype(jnp.bfloat16)
    dv_ref[...] = dv.astype(jnp.bfloat16)


def attend_call(body, causal, bounds, operands, n_out_rows):
    width = operands[0].shape[1]
    spec = [pl.BlockSpec((a.shape[0], 128), lambda i: (0, i)) for a in operands]
    return pl.pallas_call(
        functools.partial(body, causal),
        grid=(width // 128,),
        out_shape=[jax.ShapeDtypeStruct((r, width), jnp.bfloat16) for r in n_out_rows],
        in_specs=[pl.BlockSpec(memory_space=pltpu.SMEM)] + spec,
        out_specs=[pl.BlockSpec((r, 128), lambda i: (0, i)) for r in n_out_rows],
        compiler_params=pltpu.CompilerParams(vmem_limit_bytes=32 * 1024 * 1024),
        name=("self_" if causal else "cross_") + body.__name__,
    )(bounds, *operands)


def attend(causal, bounds, q, k, v):
    return attend_call(attend_body, causal, bounds, (q, k, v), [q.shape[0]])[0]


def attend_grads(causal, bounds, q, k, v, g):
    return attend_call(attend_back_body, causal, bounds, (q, k, v, g), [q.shape[0], k.shape[0], k.shape[0]])


eps_norm = 1e-05


def layer_norm(values_in, gain_vec, shift_vec):
    centre = values_in - jnp.mean(values_in, axis=-1, keepdims=True)
    spread = jnp.mean(centre * centre, axis=-1, keepdims=True)
    return centre * lax.rsqrt(spread + eps_norm) * gain_vec + shift_vec


def gelu_exact(values_in):
    return jax.nn.gelu(values_in, approximate=False)


def project(left, right):
    return jnp.einsum("gti,ij->gtj", left, right, preferred_element_type=jnp.float32)


def project_back(left, right):
    return jnp.einsum("gtj,ij->gti", left, right, preferred_element_type=jnp.float32)


def outer_sum(left, right):
    return jnp.einsum("gti,gtj->ij", left, right, preferred_element_type=jnp.float32)


ORDERS = ("zyx", "zxy") * 4 + ("zyx", "yxz", "zxy", "zyx", "xyz", "zxy", "yxz", "zyx", "xyz")
SHORT_ORDERS = ("zyx", "zxy", "zyx", "zxy", "zyx", "zxy", "yxz", "zyx", "xyz")


class Params(NamedTuple):
    w_query: jax.Array
    w_key: jax.Array
    w_value: jax.Array
    w_out: jax.Array
    c_query: jax.Array
    c_key: jax.Array
    c_value: jax.Array
    c_out: jax.Array
    w_text: jax.Array
    w_up: jax.Array
    w_down: jax.Array
    gain_attn: jax.Array
    bias_attn: jax.Array
    gain_cross: jax.Array
    bias_cross: jax.Array
    gain_feed: jax.Array
    bias_feed: jax.Array


BLOCKS, GAINS = 11, 6


def all_axes():
    return ("dp", "seq")


class Wires:
    def __init__(self, own):
        self.nz = lax.axis_size("dp") // 2
        self.rows, self.width = own.w_query.shape
        self.text_rows = own.w_text.shape[0]
        rows, width = self.rows, self.width
        up, down = own.w_up.shape[1] // width, own.w_down.shape[0] // rows
        self.units = [(g, 0, rows, 0, width) for g in range(9)]
        self.units += [(9, 0, rows, k * width, width) for k in range(up)]
        self.units += [(10, k * rows, rows, 0, width) for k in range(down)]
        self.orders = [ORDERS[i % len(ORDERS)] for i in range(len(self.units))]

    @staticmethod
    def fits(own, frames, text):
        rows, width = own.w_query.shape
        return (
            lax.axis_size("seq") == 4 and lax.axis_size("dp") % 2 == 0 and rows == 32 and width % 128 == 0
            and own.w_text.shape[0] % 8 == 0 and own.w_text.shape[0] + 8 <= rows
            and own.w_up.shape[0] == rows and own.w_up.shape[1] % width == 0
            and own.w_down.shape[0] % rows == 0 and own.w_down.shape[1] == width
            and frames.shape[0] == 1 and frames.shape[1] % 32 == 0 and text.shape[0] == 1 and text.shape[1] % 128 == 0
        )

    def gather(self, own, frames):
        gains = jnp.stack(own[BLOCKS:])
        gains = jnp.pad(gains, ((0, self.rows - self.text_rows - GAINS), (0, self.width - gains.shape[1])))
        arrays = list(own[:BLOCKS])
        arrays[8] = jnp.concatenate([own.w_text, gains], axis=0)
        *full, all_rows = gather_weights(arrays[:9], frames[0], self.units[:9], SHORT_ORDERS, self.nz)
        full += [lax.all_gather(v, all_axes(), axis=0, tiled=True) for v in arrays[9:]]
        mixed = full[8].reshape((-1, self.rows, self.width))
        full = [f.reshape((-1, f.shape[-1])) for f in full]
        full[8] = mixed[:, : self.text_rows].reshape((-1, self.width))
        gains = [mixed[:, self.text_rows + i, : own[BLOCKS + i].shape[0]].reshape((-1,)) for i in range(GAINS)]
        return Params(*full, *gains), all_rows.reshape((1, -1, self.width))

    def scatter(self, grads):
        low = [v.astype(jnp.bfloat16) for v in grads]
        shards = self.nz * 8
        rest = jnp.stack([v.reshape((shards, -1)) for v in low[BLOCKS:]], axis=1)
        rest = jnp.pad(rest, ((0, 0), (0, self.rows - self.text_rows - GAINS), (0, self.width - rest.shape[2])))
        low[8] = jnp.concatenate([low[8].reshape((shards, self.text_rows, self.width)), rest], axis=1)
        arrays = [v.reshape((self.nz, 2, 2, 2, -1, v.shape[-1])) for v in low[:BLOCKS]]
        sums = scatter_grads(arrays, self.units, self.orders, self.nz)
        *blocks, mixed = deliver(sums, self.units, self.text_rows, [a.shape[4:] for a in arrays])
        gains = [mixed[i, : v.shape[0] // shards] for i, v in enumerate(grads[BLOCKS:])]
        return Params(*blocks, *gains)

    def share(self, arrays, number):
        return [v[None] for v in share_sums([a.reshape((2, 2, -1, self.width)) for a in arrays], number)]


class PlainWires:
    def gather(self, own, frames):
        full = Params(*[lax.all_gather(v, all_axes(), axis=0, tiled=True) for v in own])
        return full, lax.all_gather(frames, "seq", axis=1, tiled=True)

    def scatter(self, grads):
        return Params(*[lax.psum_scatter(v, all_axes(), scatter_dimension=0, tiled=True) for v in grads])

    def share(self, arrays, number):
        return [lax.psum_scatter(a, "seq", scatter_dimension=1, tiled=True) for a in arrays]


def attention(causal, bounds, q, k, v):
    return attend(causal, bounds[0], q[0], k[0], v[0])[None]


def attention_back(causal, bounds, *operands):
    return [r[None] for r in attend_grads(causal, bounds[0], *[a[0] for a in operands])]


def on_device(frames, cotangent, text_states, frame_start, prompt_len, *params):
    own = Params(*params)
    low = jnp.bfloat16
    wires = Wires(own) if Wires.fits(own, frames, text_states) else PlainWires()
    full, all_frames = wires.gather(own, frames)
    wide = [v.astype(jnp.float32) for v in full[BLOCKS:]]
    frames_f = frames.astype(jnp.float32)
    frame_count = frames.shape[1]
    normed, norm_one_back = jax.vjp(layer_norm, frames_f, wide[0], wide[1])
    normed_low = normed.astype(low)
    normed_all = layer_norm(all_frames.astype(jnp.float32), wide[0], wide[1]).astype(low)
    query_rows = project(normed_low, full.w_query).astype(low)
    key_all = project(normed_all, full.w_key).astype(low)
    value_all = project(normed_all, full.w_value).astype(low)
    rank = lax.axis_index("seq")
    self_bounds = jnp.stack([jnp.full_like(frame_start, rank * frame_count), frame_start], axis=1)
    attended = attention(True, self_bounds, query_rows, key_all, value_all)
    first = frames_f + project(attended, full.w_out)
    text_count = text_states.shape[1]
    quarter = text_count // lax.axis_size("seq")
    text_start = rank * quarter
    text_part = lax.dynamic_slice_in_dim(text_states, text_start, quarter, 1)
    proj_all = project(text_states, full.w_text).astype(low)
    cross_keys = project(proj_all, full.c_key).astype(low)
    cross_values = project(proj_all, full.c_value).astype(low)
    proj_part = lax.dynamic_slice_in_dim(proj_all, text_start, quarter, 1)
    normed_two, norm_two_back = jax.vjp(layer_norm, first, wide[2], wide[3])
    normed_two_low = normed_two.astype(low)
    cross_query = project(normed_two_low, full.c_query).astype(low)
    cross_bounds = jnp.stack([prompt_len, prompt_len], axis=1)
    cross_mix = attention(False, cross_bounds, cross_query, cross_keys, cross_values)
    second = first + project(cross_mix, full.c_out)
    normed_three, norm_three_back = jax.vjp(layer_norm, second, wide[4], wide[5])
    three_low = normed_three.astype(low)
    hidden = project(three_low, full.w_up)
    activated, gelu_back = jax.vjp(gelu_exact, hidden)
    act_low = activated.astype(low)
    block_out = (second + project(act_low, full.w_down)).astype(low)
    grad_act = project_back(cotangent, full.w_down)
    dw_down = outer_sum(act_low, cotangent)
    grad_hidden = gelu_back(grad_act)[0].astype(low)
    dw_up = outer_sum(three_low, grad_hidden)
    grad_second_ln, dgain_feed, dbias_feed = norm_three_back(project_back(grad_hidden, full.w_up))
    grad_second = cotangent.astype(jnp.float32) + grad_second_ln
    second_low = grad_second.astype(low)
    dc_out = outer_sum(cross_mix, second_low)
    grad_cross_mix = project_back(second_low, full.c_out).astype(low)
    cq_low, grad_ck, grad_cv = attention_back(
        False, cross_bounds, cross_query, cross_keys, cross_values, grad_cross_mix
    )
    ck_low, cv_low = wires.share([grad_ck, grad_cv], 3)
    dc_key = outer_sum(proj_part, ck_low)
    dc_value = outer_sum(proj_part, cv_low)
    grad_proj = (project_back(ck_low, full.c_key) + project_back(cv_low, full.c_value)).astype(low)
    dw_text = outer_sum(text_part, grad_proj)
    text_grad = project_back(grad_proj, full.w_text)
    dc_query = outer_sum(normed_two_low, cq_low)
    grad_first_ln, dgain_cross, dbias_cross = norm_two_back(project_back(cq_low, full.c_query))
    grad_first = grad_second + grad_first_ln
    first_low = grad_first.astype(low)
    dw_out = outer_sum(attended, first_low)
    grad_attended = project_back(first_low, full.w_out).astype(low)
    q_low, grad_k_all, grad_v_all = attention_back(
        True, self_bounds, query_rows, key_all, value_all, grad_attended
    )
    k_low, v_low = wires.share([grad_k_all, grad_v_all], 4)
    dw_query = outer_sum(normed_low, q_low)
    dw_key = outer_sum(normed_low, k_low)
    dw_value = outer_sum(normed_low, v_low)
    grad_normed = (
        project_back(q_low, full.w_query) + project_back(k_low, full.w_key) + project_back(v_low, full.w_value)
    )
    grad_frames_ln, dgain_attn, dbias_attn = norm_one_back(grad_normed)
    frames_grad = (grad_first + grad_frames_ln).astype(low)
    sums = wires.scatter(
        Params(
            dw_query, dw_key, dw_value, dw_out, dc_query, dc_key, dc_value, dc_out, dw_text, dw_up, dw_down,
            dgain_attn, dbias_attn, dgain_cross, dbias_cross, dgain_feed, dbias_feed,
        )
    )
    return (block_out, frames_grad, text_grad, *sums)


def solution(mesh):
    both = P(all_axes(), None)
    rows, vector = P(*all_axes(), None), P(all_axes())
    item, whole = P("dp"), P("dp", None, None)
    return jax.shard_map(
        on_device,
        mesh=mesh,
        in_specs=(rows, rows, whole, item, item) + (both,) * BLOCKS + (vector,) * GAINS,
        out_specs=(rows,) * 3 + (both,) * BLOCKS + (vector,) * GAINS,
        check_vma=False,
    )
```

time: 2480 us -> 485 us (0.20)
  waiting for transfers between devices: 2130 us -> 1.54 us
  Pallas kernels: 0 us -> 334 us
  blocking collectives: 82.4 us -> 0 us
  matrix products: 155 us -> 78.2 us
  local copies, waits for them, and re-layouts: 70.3 us -> 31.1 us
    reduce_scatter x11 -> x0, waiting for transfers between devices: 1510 us -> none  [the longest x1 187 us: on_device(): lax.psum_scatter(dw_down, ('dp', 'seq'), scatter_dimension=0, tiled=True)]
    all_gather x13 -> x2, waiting for transfers between devices: 611 us -> 0.16 us  [gather(): lax.all_gather(v, all_axes(), axis=0, tiled=True)]
    pallas_call x0 -> x9, Pallas kernels: none -> 334 us  [the longest x1 138 us: scatter_grads(): pl.pallas_call(functools.partial(scatter_body, nz, units, slots, n, depth...]
    unnamed x2 -> x0, blocking collectives: 82.4 us -> none
    unnamed x114 -> x158, local copies, waits for them, and re-layouts: 61.6 us -> 26 us
    dot_general x10 -> x0, matrix products: 32.2 us -> none  [the longest x2 8.53 us: attend_back(): jnp.einsum('gqhd,gkhd->ghqk', grad_heads, value_heads, preferred_element_...]
  transfers between devices with their start and end apart: 28 -> 2, of which waited for: 25 -> 1; matrix products, arithmetic and copies ran while one was open for 8% -> 6% of each run, Pallas kernels for 0% -> 29%
where the time goes in v1:
time: 485 us; the launch traced here: 476 us
  Pallas kernels  334 us (69%)
  matrix products  78.2 us (16%)
  local copies, waits for them, and re-layouts  31.1 us (6%)
  between operations  16.6 us (3%)
  other arithmetic  14.1 us (3%)
    pallas_call x1, Pallas kernels, scatter_grads(): pl.pallas_call(functools.partial(scatter_body, nz, units, slots, n, depth...  138 us
    pallas_call x1, Pallas kernels, gather_weights(): pl.pallas_call(functools.partial(gather_body, nz, units, slots, n, depth)...  120 us
    pallas_call x4, Pallas kernels, attend_call(): pl.pallas_call(functools.partial(body, causal), grid=(width // 128,), out...  46 us
    dot_general x11, matrix products, outer_sum(): jnp.einsum('gti,gtj->ij', left, right, preferred_element_type=jnp.float32)  31.4 us
    pallas_call x2, Pallas kernels, share_sums(): pl.pallas_call(functools.partial(share_body, n, chunk), out_shape=[jax.Sh...  28.8 us
    unnamed x158, local copies, waits for them, and re-layouts  26 us
    dot_general x11, matrix products, project(): jnp.einsum('gti,ij->gtj', left, right, preferred_element_type=jnp.float32)  24.8 us
    dot_general x11, matrix products, project_back(): jnp.einsum('gtj,ij->gti', left, right, preferred_element_type=jnp.float32)  22 us
  transfers between devices with their start and end apart: 2, of which 1 were waited for; matrix products, arithmetic and copies ran while one was open for 6% of the time, Pallas kernels for 29%

profile of v1, /device:TPU:0, one launch (start us, length us, event | category | flops | bytes accessed | tf_op | source)
XLA Modules:
  0.0 475.8 jit_solution(17955184647523134804)
XLA Ops:
  10.0 0.8 stack.45
  10.8 0.8 fusion.46.refs_8_
  11.6 1.0 copy-done.1
  12.5 0.8 copy-done.44
  13.4 0.8 copy-done.45
  14.2 0.8 copy-done.46
  15.1 0.8 copy-done.47
  15.9 0.8 copy-done.48
  16.7 0.8 copy-done.49
  17.6 0.8 copy-done.50
  18.4 0.8 copy-done.51
  19.2 120.0 %gather_weights.1 = (bf16[4,2,2,2,32,1024]{5,4,3,2,1,0:T(8,128)(2,1)S(1)}, bf16[4,2,2,2,32,1024]{5,4,3,2,1,0:T(8,128)(2,1)S(1)}, bf16[4,2,2,2,32,1024]{5,4,3,2,1...) custom-call(bf16[32,1024]{1,0:T(8,128)(2,1)S(1)} %copy-done.44, ...), custom_call_target="tpu_custom_call" | custom-call | tf_op jit(solution)/shard_map/gather_weights/pallas_call | solution.py:232
  139.3 1.3 copy-done.4
  140.6 1.3 copy-done.6
  141.9 1.3 copy-done.9
  143.2 1.3 copy-done.18
  144.6 1.3 copy-done.21
  145.9 1.4 copy-done.24
  147.3 1.3 copy-done.27
  148.6 1.4 copy-done.30
  150.0 1.3 copy-done.37
  152.3 2.7 slice.56
  155.0 1.6 fusion.48
  159.4 1.5 convolution_convert_fusion.11.v_ref
  161.0 1.5 convolution_convert_fusion.12.k_ref
  162.6 10.4 %self_attend_body.1 = bf16[160,1024]{1,0:T(8,128)(2,1)S(1)} custom-call(s32[2]{0:T(128)S(1)} %add_bitcast_fusion.bounds_ref, bf16[160,1024]{1,0:T(8,128)(2,1)S(1)} %convolution_convert_fusion.19.q_ref, bf16[640,1024]{1,0:T(8,128)(2,1)S(1)} %convolution_convert_fusion.12.k_ref, bf16[640,1024]{1,0:T(8,128)(2,1)S(1)} %convolution_convert_fusion.11.v_ref), custom_call_target="tpu_custom_call" | custom-call | tf_op jit(solution)/shard_map/self_attend_body/pallas_call | solution.py:498
  177.8 7.6 %cross_attend_body.1 = bf16[160,1024]{1,0:T(8,128)(2,1)S(1)} custom-call(s32[2]{0:T(128)S(1)} %add_bitcast_fusion.1.bounds_ref, bf16[160,1024]{1,0:T(8,128)(2,1)S(1)} %convolution_convert_fusion.18.q_ref, bf16[256,1024]{1,0:T(8,128)(2,1)S(1)} %convolution_convert_fusion.14.k_ref, bf16[256,1024]{1,0:T(8,128)(2,1)S(1)} %convolution_convert_fusion.13.v_ref), custom_call_target="tpu_custom_call" | custom-call | tf_op jit(solution)/shard_map/cross_attend_body/pallas_call | solution.py:498
  186.1 0.8 copy-done.54
  187.2 11.7 %multiply_convert_fusion = (bf16[160,4096]{1,0:T(8,128)(2,1)}, f32[160,4096]{1,0:T(8,128)}, f32[160,4096]{1,0:T(8,128)}) fusion(bf16[1024,4096]{1,0:T(8,128)(2,1)} %all-gather.3.cloned.1.call-done, f32[1,160,1024]{2,1,0:T(8,128)} %copy-done.54, f32[1024]{0:T(1024)S(1)} %reshape.823, f32[1024]{0:T(1024)S(1)} %reshape.822, f32[160]{0:T(256)S(1)} %fusion.55, ...), kind=kOutput, calls=%fused_computation.5 | convolution fusion | flops 1385594880 | bytes 15607040 | tf_op jit(solution)/shard_map/gti,ij->gtj/dot_general | solution.py:531
  199.1 8.5 %add_convert_fusion = bf16[160,4096]{1,0:T(8,128)(2,1)S(1)} fusion(f32[160,4096]{1,0:T(8,128)} %get-tuple-element.101, f32[160,4096]{1,0:T(8,128)} %get-tuple-element.112, bf16[4096,1024]{1,0:T(8,128)(2,1)} %all-gather.5.cloned.1.call-done, bf16[1,160,1024]{2,1,0:T(8,128)(2,1)} %param.23), kind=kOutput, calls=%fused_computation.4 | convolution fusion | flops 1351352320 | bytes 15269888 | tf_op jit(solution)/shard_map/gtj,ij->gti/dot_general | solution.py:535
  207.7 3.1 fusion.22
  212.9 0.8 convolution_convert_fusion.17.g_ref
  213.7 11.3 %cross_attend_back_body.1 = (bf16[160,1024]{1,0:T(8,128)(2,1)S(1)}, bf16[256,1024]{1,0:T(8,128)(2,1)S(1)}, bf16[256,1024]{1,0:T(8,128)(2,1)S(1)}) custom-call(s32[2]{0:T(128)S(1)} %add_bitcast_fusion.1.bounds_ref, bf16[160,1024]{1,0:T(8,128)(2,1)S(1)} %convolution_convert_fusion.18.q_ref, bf16[256,1024]{1,0:T(8,128)(2,1)S(1)} %copy-done.36, ...), custom_call_target="tpu_custom_call" | custom-call | tf_op jit(solution)/shard_map/cross_attend_back_body/pallas_call | solution.py:498
  225.1 2.3 fusion.23
  227.4 2.2 convolution_convert_fusion.5
  229.6 1.1 reduce_sum.209
  231.4 1.1 reduce_sum.204
  232.5 1.6 fusion.69
  234.2 1.3 add_add_fusion.3
  235.5 0.9 convolution_convert_fusion.16.g_ref
  236.4 2.1 convolution_convert_fusion.6
  238.5 2.1 convolution_convert_fusion.2
  240.6 16.7 %self_attend_back_body.1 = (bf16[160,1024]{1,0:T(8,128)(2,1)S(1)}, bf16[640,1024]{1,0:T(8,128)(2,1)S(1)}, bf16[640,1024]{1,0:T(8,128)(2,1)S(1)}) custom-call(s32[2]{0:T(128)S(1)} %add_bitcast_fusion.bounds_ref, bf16[160,1024]{1,0:T(8,128)(2,1)S(1)} %copy-done.39, bf16[640,1024]{1,0:T(8,128)(2,1)S(1)} %copy-done.15, bf16[640,1024]{1,0:T(8,128)(2,1)S(1)} %copy-done.13, ...), custom_call_target="tpu_custom_call" | custom-call | tf_op jit(solution)/shard_map/self_attend_back_body/pallas_call | solution.py:498
  257.4 1.7 fusion.74
  259.0 2.2 convolution_convert_fusion.9
  261.2 10.0 %share_sums.3 = (bf16[64,1024]{1,0:T(8,128)(2,1)S(1)}, bf16[64,1024]{1,0:T(8,128)(2,1)S(1)}) custom-call(bf16[2,2,64,1024]{3,2,1,0:T(8,128)(2,1)S(1)} %bitcast.213, bf16[2,2,64,1024]{3,2,1,0:T(8,128)(2,1)S(1)} %bitcast.214), custom_call_target="tpu_custom_call" | custom-call | tf_op jit(solution)/shard_map/share_sums/pallas_call | solution.py:415
  272.0 0.8 fusion.10
  272.8 1.3 convolution_bitcast_fusion.3
  274.1 1.8 convolution_convert_fusion.10
  275.8 2.0 convolution_convert_fusion.3
  277.9 2.1 convolution_convert_fusion.4
  280.0 5.7 %convolution_convert_fusion.1 = bf16[1024,4096]{1,0:T(8,128)(2,1)} fusion(bf16[160,4096]{1,0:T(8,128)(2,1)S(1)} %copy-done.68, f32[1,160,1024]{2,1,0:T(8,128)S(1)} %copy-done.56, f32[1024]{0:T(1024)S(1)} %reshape.823, f32[1024]{0:T(1024)S(1)} %reshape.822, f32[160]{0:T(256)S(1)} %fusion.55, f32[160]{0:T(256)S(1)} %broadcast_multiply_fusion.1), kind=kOutput, calls=%fused_computation.1 | convolution fusion | flops 1347190784 | bytes 10364160 | tf_op jit(solution)/shard_map/gti,gtj->ij/dot_general | solution.py:539
  285.8 18.8 %share_sums.2 = (bf16[160,1024]{1,0:T(8,128)(2,1)S(1)}, bf16[160,1024]{1,0:T(8,128)(2,1)S(1)}) custom-call(bf16[2,2,160,1024]{3,2,1,0:T(8,128)(2,1)S(1)} %bitcast.211, bf16[2,2,160,1024]{3,2,1,0:T(8,128)(2,1)S(1)} %bitcast.212), custom_call_target="tpu_custom_call" | custom-call | tf_op jit(solution)/shard_map/share_sums/pallas_call | solution.py:415
  304.6 2.2 convolution_convert_fusion.8
  306.8 0.8 convolution_add_fusion.1
  307.7 2.2 convolution_convert_fusion.7
  309.9 1.0 fusion.21
  311.4 1.0 add_convert_fusion.2
  312.8 7.0 %convolution_convert_fusion = bf16[4096,1024]{1,0:T(8,128)(2,1)} fusion(bf16[160,4096]{1,0:T(8,128)(2,1)S(1)} %copy-done.60, bf16[1,160,1024]{2,1,0:T(8,128)(2,1)} %param.23), kind=kOutput, calls=%fused_computation | convolution fusion | flops 1346371584 | bytes 10027008 | tf_op jit(solution)/shard_map/gti,gtj->ij/dot_general | solution.py:539
  319.8 1.6 pad_maximum_fusion.refs_8_
  321.5 137.7 %scatter_grads.1.sums = f32[17,32,1024]{2,1,0:T(8,128)} custom-call(bf16[4,2,2,2,32,1024]{5,4,3,2,1,0:T(8,128)(2,1)} %bitcast.225, bf16[4,2,2,2,32,1024]{5,4,3,2,1,0:T(8,128)(2,1)} %bitcast.226, bf16[4,2,2,2,32,1024]{5,4,3,2,1,0:T(8,128)(2,1)} %bitcast.227, bf16[4,2,2,2,32,1024]{5,4,3,2,1,0:T(8,128)(2,1)} %bitcast.222, ...), custom_call_target="tpu_custom_call" | custom-call | tf_op jit(solution)/shard_map/scatter_grads/pallas_call | solution.py:343
  459.2 1.6 copy-done.3
  460.9 1.5 deliver.1
  462.9 5.6 %fusion.9 = bf16[1,160,1024]{2,1,0:T(8,128)(2,1)} fusion(f32[1,160,1024]{2,1,0:T(8,128)S(1)} %copy-done.57, bf16[160,4096]{1,0:T(8,128)(2,1)S(1)} %copy-done.60, bf16[4096,1024]{1,0:T(8,128)(2,1)} %all-gather.5.cloned.1.call-done), kind=kOutput, calls=%fused_computation.45 | convolution fusion | flops 1342504960 | bytes 10682368 | tf_op jit(solution)/shard_map/gti,ij->gtj/dot_general | solution.py:531
  (196 shorter events, 16.2 us)
Async XLA Ops:
  7.2 166.7 %copy-start = (bf16[1,256,768]{2,1,0:T(8,128)(2,1)S(1)}, bf16[1,256,768]{2,1,0:T(8,128)(2,1)}, u32[]{:S(2)}) copy-start(bf16[1,256,768]{2,1,0:T(8,128)(2,1)} %param.24) | copy-start | bytes 1179652
  7.2 180.0 %all-gather.3.cloned.1.call-start = ((), (), s32[]{:S(2)}) async-start(), calls=%async_computation | async-start | bytes 8650752 | tf_op jit(solution)/shard_map/all_gather | solution.py:602
  7.9 191.2 %all-gather.5.cloned.1.call-start = ((), (), s32[]{:S(2)}) async-start(), calls=%async_computation.1 | async-start | bytes 8650752 | tf_op jit(solution)/shard_map/all_gather | solution.py:602
  139.3 1.3 copy-start.4
  140.6 1.3 copy-start.6
  141.9 1.3 copy-start.9
  143.2 1.3 copy-start.18
  144.6 1.3 copy-start.21
  145.9 1.4 copy-start.24
  147.3 1.3 copy-start.27
  148.6 1.4 copy-start.30
  150.0 1.3 copy-start.37
  151.6 5.5 %copy-start.2 = (bf16[1,160,1024]{2,1,0:T(8,128)(2,1)S(1)}, bf16[1,160,1024]{2,1,0:T(8,128)(2,1)}, u32[]{:S(2)}) copy-start(bf16[1,160,1024]{2,1,0:T(8,128)(2,1)} %param.22) | copy-start | bytes 983044
  157.0 1.6 copy-start.28
  157.5 1.9 copy-start.31
  159.2 3.3 copy-start.38
  159.4 1.6 copy-start.19
  160.9 1.6 copy-start.12
  162.6 11.1 %copy-start.14 = (bf16[640,1024]{1,0:T(8,128)(2,1)}, bf16[640,1024]{1,0:T(8,128)(2,1)S(1)}, u32[]{:S(2)}) copy-start(bf16[640,1024]{1,0:T(8,128)(2,1)S(1)} %convolution_convert_fusion.12.k_ref) | copy-start | bytes 3932164
  162.6 10.5 %copy-start.5 = (bf16[4,2,2,2,32,1024]{5,4,3,2,1,0:T(8,128)(2,1)S(1)}, bf16[4,2,2,2,32,1024]{5,4,3,2,1,0:T(8,128)(2,1)}, u32[]{:S(2)}) copy-start(bf16[4,2,2,2,32,1024]{5,4,3,2,1,0:T(8,128)(2,1)} %copy-done.4) | copy-start | bytes 6291460
  173.0 1.4 copy-start.58
  173.0 2.3 copy-start.7
  173.7 11.7 %copy-start.52 = (f32[1,160,1024]{2,1,0:T(8,128)}, f32[1,160,1024]{2,1,0:T(8,128)S(1)}, u32[]{:S(2)}) copy-start(f32[1,160,1024]{2,1,0:T(8,128)S(1)} %get-tuple-element.109) | copy-start | bytes 1966084
  174.4 1.9 copy-start.22
  174.9 2.0 copy-start.74
  175.3 1.7 copy-start.25
  177.0 9.1 %copy-start.33 = (bf16[256,1024]{1,0:T(8,128)(2,1)}, bf16[256,1024]{1,0:T(8,128)(2,1)S(1)}, u32[]{:S(2)}) copy-start(bf16[256,1024]{1,0:T(8,128)(2,1)S(1)} %convolution_convert_fusion.13.v_ref) | copy-start | bytes 1572868
  177.0 8.4 %copy-start.10 = (bf16[4,2,2,2,32,1024]{5,4,3,2,1,0:T(8,128)(2,1)S(1)}, bf16[4,2,2,2,32,1024]{5,4,3,2,1,0:T(8,128)(2,1)}, u32[]{:S(2)}) copy-start(bf16[4,2,2,2,32,1024]{5,4,3,2,1,0:T(8,128)(2,1)} %copy-done.9) | copy-start | bytes 6291460
  177.8 8.3 %copy-start.35 = (bf16[256,1024]{1,0:T(8,128)(2,1)}, bf16[256,1024]{1,0:T(8,128)(2,1)S(1)}, u32[]{:S(2)}) copy-start(bf16[256,1024]{1,0:T(8,128)(2,1)S(1)} %convolution_convert_fusion.14.k_ref) | copy-start | bytes 1572868
  199.1 8.6 %copy-start.55 = (f32[1,160,1024]{2,1,0:T(8,128)S(1)}, f32[1,160,1024]{2,1,0:T(8,128)}, u32[]{:S(2)}) copy-start(f32[1,160,1024]{2,1,0:T(8,128)} %copy-done.54) | copy-start | bytes 1966084
  199.1 8.6 %copy-start.63 = (bf16[1024,4096]{1,0:T(8,128)(2,1)S(1)}, bf16[1024,4096]{1,0:T(8,128)(2,1)}, u32[]{:S(2)}) copy-start(bf16[1024,4096]{1,0:T(8,128)(2,1)} %all-gather.3.cloned.1.call-done) | copy-start | bytes 25165828
  207.7 3.1 copy-start.67
  207.7 4.0 copy-start.69
  210.8 2.1 copy-start.11
  210.8 2.9 copy-start.34
  210.8 2.9 copy-start.36
  211.7 13.4 %copy-start.8 = (bf16[4,2,2,2,32,1024]{5,4,3,2,1,0:T(8,128)(2,1)S(1)}, bf16[4,2,2,2,32,1024]{5,4,3,2,1,0:T(8,128)(2,1)}, u32[]{:S(2)}) copy-start(bf16[4,2,2,2,32,1024]{5,4,3,2,1,0:T(8,128)(2,1)} %copy-done.6) | copy-start | bytes 6291460
  211.7 13.4 %copy-start.53 = (f32[1,160,1024]{2,1,0:T(8,128)S(1)}, f32[1,160,1024]{2,1,0:T(8,128)}, u32[]{:S(2)}) copy-start(f32[1,160,1024]{2,1,0:T(8,128)} %copy-done.52) | copy-start | bytes 1966084
  225.0 2.4 copy-start.40
  225.0 2.4 copy-start.42
  227.4 6.8 %copy-start.70 = (bf16[1,160,1024]{2,1,0:T(8,128)(2,1)S(1)}, bf16[1,160,1024]{2,1,0:T(8,128)(2,1)}, u32[]{:S(2)}) copy-start(bf16[1,160,1024]{2,1,0:T(8,128)(2,1)} %param.23) | copy-start | bytes 983044
  235.5 3.0 copy-start.61
  235.5 3.0 copy-start.17
  235.5 3.0 copy-start.72
  236.4 4.2 copy-start.13
  236.4 4.2 copy-start.15
  236.4 4.2 copy-start.39
  238.5 18.8 %copy-start.29 = (bf16[4,2,2,2,32,1024]{5,4,3,2,1,0:T(8,128)(2,1)S(1)}, bf16[4,2,2,2,32,1024]{5,4,3,2,1,0:T(8,128)(2,1)}, u32[]{:S(2)}) copy-start(bf16[4,2,2,2,32,1024]{5,4,3,2,1,0:T(8,128)(2,1)} %copy-done.27) | copy-start | bytes 6291460
  257.3 3.9 copy-start.41
  257.3 3.9 copy-start.43
  257.3 13.9 %copy-start.26 = (bf16[4,2,2,2,32,1024]{5,4,3,2,1,0:T(8,128)(2,1)S(1)}, bf16[4,2,2,2,32,1024]{5,4,3,2,1,0:T(8,128)(2,1)}, u32[]{:S(2)}) copy-start(bf16[4,2,2,2,32,1024]{5,4,3,2,1,0:T(8,128)(2,1)} %copy-done.24) | copy-start | bytes 6291460
  259.0 13.0 %copy-start.23 = (bf16[4,2,2,2,32,1024]{5,4,3,2,1,0:T(8,128)(2,1)S(1)}, bf16[4,2,2,2,32,1024]{5,4,3,2,1,0:T(8,128)(2,1)}, u32[]{:S(2)}) copy-start(bf16[4,2,2,2,32,1024]{5,4,3,2,1,0:T(8,128)(2,1)} %copy-done.21) | copy-start | bytes 6291460
  271.2 1.6 copy-start.59
  272.0 3.8 copy-start.75
  275.8 4.1 copy-start.56
  275.8 4.1 copy-start.68
  285.8 21.0 %copy-start.20 = (bf16[4,2,2,2,32,1024]{5,4,3,2,1,0:T(8,128)(2,1)S(1)}, bf16[4,2,2,2,32,1024]{5,4,3,2,1,0:T(8,128)(2,1)}, u32[]{:S(2)}) copy-start(bf16[4,2,2,2,32,1024]{5,4,3,2,1,0:T(8,128)(2,1)} %copy-done.18) | copy-start | bytes 6291460
  285.8 21.0 %copy-start.73 = (f32[160,1024]{1,0:T(8,128)S(1)}, f32[160,1024]{1,0:T(8,128)}, u32[]{:S(2)}) copy-start(f32[160,1024]{1,0:T(8,128)} %fusion.74) | copy-start | bytes 1966084
  306.8 3.0 copy-start.32
  309.9 1.5 copy-start.62
  310.9 1.9 copy-start.60
  312.8 7.1 %copy-start.64 = (bf16[768,1024]{1,0:T(8,128)(2,1)S(1)}, bf16[768,1024]{1,0:T(8,128)(2,1)}, u32[]{:S(2)}) copy-start(bf16[768,1024]{1,0:T(8,128)(2,1)} %convolution_convert_fusion.10) | copy-start | bytes 4718596
  459.2 1.6 copy-start.3
  460.9 2.0 copy-start.57
  (14 other events, 11.7 us)
Sparse Core Ops, SparseCore 0:
  10.9 108.6 all-gather.2
  122.4 76.6 all-gather.4

commit v2 on v1

--- a/solution.py
+++ b/solution.py
@@ -245,7 +245,7 @@
             pltpu.SemaphoreType.DMA((3,)),
             pltpu.SemaphoreType.DMA((3,)),
         ],
-        compiler_params=pltpu.CompilerParams(collective_id=1, has_side_effects=True, vmem_limit_bytes=16 * 1024 * 1024),
+        compiler_params=pltpu.CompilerParams(collective_id=1, has_side_effects=True, vmem_limit_bytes=VMEM_LIMIT),
         name="gather_weights",
     )(*arrays, frame_rows)
 
@@ -253,10 +253,8 @@
 BACK = (DOWN, UP, YY, XX)
 
 
-def scatter_body(nz, units, slots, n, depth, *refs):
-    ins, out = refs[:n], refs[n]
-    total, twin, landed, send_sem, recv_sem, core_send, core_recv, local_sem = refs[n + 1:]
-    here = Place(nz)
+def scatter_steps(here, units, slots, depth, ins, total, twin, landed, send_sem, recv_sem, core_send, core_recv, local_sem):
+    nz = here.nz
     z, y, x, c = here.z, here.y, here.x, here.c
     steps = slots[::-1]
     numbers, order = {}, []
@@ -267,17 +265,21 @@
             if op[0] not in order:
                 order.append(op[0])
 
-    def plane(u, which):
-        g, r0, rn, c0, cn = units[u]
+    def plane(u, b, which):
+        g, r0, rn, c0, cn = units[u][b]
         return ins[g].at[:, :, :, which, pl.ds(r0, rn), pl.ds(c0, cn)]
 
-    def local(u):
-        return pltpu.make_async_copy(plane(u, c), total.at[u], local_sem.at[u])
-
-    def across(u):
+    def rows_of(buffer, u, b):
+        rn = units[u][b][2]
+        return buffer.at[u, :, :, :, pl.ds(b * rn, rn)]
+
+    def local(u, b):
+        return pltpu.make_async_copy(plane(u, b, c), rows_of(total, u, b), local_sem.at[u, b])
+
+    def across(u, b):
         return pltpu.make_async_remote_copy(
-            src_ref=plane(u, 1 - c), dst_ref=twin.at[u], send_sem=core_send.at[u], recv_sem=core_recv.at[u],
-            device_id=here.device[CORE], device_id_type=MESH,
+            src_ref=plane(u, b, 1 - c), dst_ref=rows_of(twin, u, b), send_sem=core_send.at[u, b],
+            recv_sem=core_recv.at[u, b], device_id=here.device[CORE], device_id_type=MESH,
         )
 
     def remote(u, way, t, p):
@@ -287,15 +289,25 @@
             device_id=here.device[BACK[way]], device_id_type=MESH,
         )
 
-    for u in order:
-        local(u).start()
+    ahead = 3
+    blocks = range(len(units[0]))
+    for u in order[:ahead]:
+        for b in blocks:
+            local(u, b).start()
     here.greet()
-    for u in order:
-        across(u).start()
+    for u in order[:ahead]:
+        for b in blocks:
+            across(u, b).start()
 
     def join(u):
-        local(u).wait()
-        across(u).wait_recv()
+        later = order.index(u) + ahead
+        if later < len(order):
+            for b in blocks:
+                local(order[later], b).start()
+                across(order[later], b).start()
+        for b in blocks:
+            local(u, b).wait()
+            across(u, b).wait_recv()
 
         @pl.loop(0, nz)
         def _(a):
@@ -325,36 +337,56 @@
                             total[u, p[0], p[1], p[2]].astype(jnp.float32) + landed[i].astype(jnp.float32)
                         ).astype(jnp.bfloat16)
                     when(cond, add)
-    for u in range(len(units)):
-        out[u] = total[u, z, y, x].astype(jnp.float32)
+        yield t
     for t, slot in enumerate(steps):
         for axis, (u, _, j, fy, fx) in slot.items():
             for way, cond, p in here.gather_moves(axis, j, fy, fx)[1]:
                 when(cond, lambda u=u, way=way, p=p: remote(u, way, t, p).wait_send())
     for u in order:
-        across(u).wait_send()
+        for b in blocks:
+            across(u, b).wait_send()
+
+
+def unit_shape(units):
+    return sum(block[2] for block in units[0]), units[0][0][4]
+
+
+def scatter_scratch(units, slots, nz):
+    rows, columns = unit_shape(units)
+    count = sum(len(WAYS_OF[axis]) for slot in slots for axis in slot)
+    plane = (len(units), nz, 2, 2, rows, columns)
+    return [
+        pltpu.VMEM(plane, jnp.bfloat16),
+        pltpu.VMEM(plane, jnp.bfloat16),
+        pltpu.VMEM((count, rows, columns), jnp.bfloat16),
+        pltpu.SemaphoreType.DMA((count,)),
+        pltpu.SemaphoreType.DMA((count,)),
+        pltpu.SemaphoreType.DMA((len(units), len(units[0]))),
+        pltpu.SemaphoreType.DMA((len(units), len(units[0]))),
+        pltpu.SemaphoreType.DMA((len(units), len(units[0]))),
+    ]
+
+
+def scatter_body(nz, units, slots, n, depth, *refs):
+    ins, out = refs[:n], refs[n]
+    here = Place(nz)
+    for _ in scatter_steps(here, units, slots, depth, ins, *refs[n + 1:]):
+        pass
+    total = refs[n + 1]
+    for u in range(len(units)):
+        out[u] = total[u, here.z, here.y, here.x].astype(jnp.float32)
 
 
 def scatter_grads(arrays, units, perms, nz, depth=2):
     n = len(arrays)
     slots = make_schedule(perms, nz, lag=depth + 1)
-    count = sum(2 if axis == "z" else 1 for slot in slots for axis in slot)
-    rows, columns = units[0][2], units[0][4]
+    rows, columns = unit_shape(units)
     return pl.pallas_call(
         functools.partial(scatter_body, nz, units, slots, n, depth),
         out_shape=jax.ShapeDtypeStruct((len(units), rows, columns), jnp.float32),
         in_specs=[pl.BlockSpec(memory_space=pl.ANY)] * n,
         out_specs=pl.BlockSpec(memory_space=pltpu.VMEM),
-        scratch_shapes=[
-            pltpu.VMEM((len(units), nz, 2, 2, rows, columns), jnp.bfloat16),
-            pltpu.VMEM((len(units), nz, 2, 2, rows, columns), jnp.bfloat16),
-            pltpu.VMEM((count, rows, columns), jnp.bfloat16),
-            pltpu.SemaphoreType.DMA((count,)),
-            pltpu.SemaphoreType.DMA((count,)),
-            pltpu.SemaphoreType.DMA((len(units),)),
-            pltpu.SemaphoreType.DMA((len(units),)),
-            pltpu.SemaphoreType.DMA((len(units),)),
-        ],
+        scratch_shapes=scatter_scratch(units, slots, nz),
         compiler_params=pltpu.CompilerParams(collective_id=2, has_side_effects=True, vmem_limit_bytes=VMEM_LIMIT),
         name="scatter_grads",
     )(*arrays)
@@ -426,23 +458,26 @@
     )(*arrays)
 
 
-def deliver_body(units, text_rows, sums, *outs):
-    for u, (g, r0, rn, c0, cn) in enumerate(units):
-        if g == 8:
-            outs[g][...] = sums[u, :text_rows]
-            outs[-1][...] = sums[u, text_rows:text_rows + 8]
-        else:
-            outs[g][r0:r0 + rn, c0:c0 + cn] = sums[u]
-
-
-def deliver(sums, units, text_rows, shapes):
-    shapes = [(text_rows,) + s[1:] if g == 8 else s for g, s in enumerate(shapes)] + [(8, sums.shape[2])]
+def deliver_body(parts, text_rows, n, *refs):
+    ins, outs = refs[:n], refs[n:]
+    for sums, units in zip(ins, parts):
+        for u, unit in enumerate(units):
+            for b, (g, r0, rn, c0, cn) in enumerate(unit):
+                if g == 8:
+                    outs[g][...] = sums[u, :text_rows]
+                    outs[-1][...] = sums[u, text_rows:text_rows + 8]
+                else:
+                    outs[g][r0:r0 + rn, c0:c0 + cn] = sums[u, b * rn:(b + 1) * rn]
+
+
+def deliver(sums, parts, text_rows, shapes):
+    shapes = [(text_rows,) + s[1:] if g == 8 else s for g, s in enumerate(shapes)] + [(8, sums[0].shape[2])]
     return pl.pallas_call(
-        functools.partial(deliver_body, units, text_rows),
-        out_shape=[jax.ShapeDtypeStruct(s, sums.dtype) for s in shapes],
+        functools.partial(deliver_body, parts, text_rows, len(sums)),
+        out_shape=[jax.ShapeDtypeStruct(s, jnp.float32) for s in shapes],
         compiler_params=pltpu.CompilerParams(vmem_limit_bytes=16 * 1024 * 1024),
         name="deliver",
-    )(sums)
+    )(*sums)
 
 
 def pair_scores(bounds_ref, q, k, keep, causal):
@@ -514,6 +549,244 @@
     return attend_call(attend_back_body, causal, bounds, (q, k, v, g), [q.shape[0], k.shape[0], k.shape[0]])
 
 
+def dot_tt(a, b):
+    return lax.dot_general(a, b, (((0,), (0,)), ((), ())), preferred_element_type=jnp.float32)
+
+
+def dot_nt(a, b):
+    return lax.dot_general(a, b, (((1,), (1,)), ((), ())), preferred_element_type=jnp.float32)
+
+
+def norm_parts(v):
+    centre = v - jnp.mean(v, axis=1, keepdims=True)
+    rate = lax.rsqrt(jnp.mean(centre * centre, axis=1, keepdims=True) + eps_norm)
+    return centre * rate, rate
+
+
+def norm_grads(v, gain, h):
+    xh, rate = norm_parts(v)
+    hg = h * gain
+    dv = (hg - jnp.mean(hg, axis=1, keepdims=True) - xh * jnp.mean(hg * xh, axis=1, keepdims=True)) * rate
+    return dv, jnp.sum(h * xh, axis=0, keepdims=True), jnp.sum(h, axis=0, keepdims=True)
+
+
+class Share:
+    def __init__(self, here, mine, twins, sums, landed, core_send, core_recv, x_send, x_recv, chunk):
+        self.here, self.mine, self.twins, self.sums, self.landed = here, mine, twins, sums, landed
+        self.sems, self.chunk = (core_send, core_recv, x_send, x_recv), chunk
+
+    def columns(self, k):
+        return pl.ds(k * self.chunk, self.chunk)
+
+    def across(self, g, k, far):
+        here, f = self.here, 1 if far else 0
+        part = (1 - here.x if far else here.x) * 2 + 1 - here.c
+        return pltpu.make_async_remote_copy(
+            src_ref=self.mine[g].at[part, :, self.columns(k)], dst_ref=self.twins[g].at[f, :, self.columns(k)],
+            send_sem=self.sems[0].at[f, g, k], recv_sem=self.sems[1].at[f, g, k],
+            device_id=here.device[CORE], device_id_type=MESH,
+        )
+
+    def beyond(self, g, k):
+        return pltpu.make_async_remote_copy(
+            src_ref=self.sums[g].at[:, self.columns(k)], dst_ref=self.landed[g].at[:, self.columns(k)],
+            send_sem=self.sems[2].at[g, k], recv_sem=self.sems[3].at[g, k],
+            device_id=self.here.device[XX], device_id_type=MESH,
+        )
+
+    def send(self, k):
+        for far in (True, False):
+            for g in range(len(self.mine)):
+                self.across(g, k, far).start()
+
+    def forward(self, k):
+        here, cols = self.here, slice(k * self.chunk, (k + 1) * self.chunk)
+        for g, mine in enumerate(self.mine):
+            self.across(g, k, True).wait_recv()
+            part = (1 - here.x) * 2 + here.c
+            self.sums[g][:, cols] = (
+                mine[part, :, cols].astype(jnp.float32) + self.twins[g][1, :, cols].astype(jnp.float32)
+            ).astype(jnp.bfloat16)
+            self.beyond(g, k).start()
+
+    def collect(self, g, k):
+        here, cols = self.here, slice(k * self.chunk, (k + 1) * self.chunk)
+        self.across(g, k, False).wait_recv()
+        self.beyond(g, k).wait_recv()
+        return (
+            self.mine[g][here.x * 2 + here.c, :, cols].astype(jnp.float32) + self.twins[g][0, :, cols].astype(jnp.float32)
+            + self.landed[g][:, cols].astype(jnp.float32)
+        ).astype(jnp.bfloat16)
+
+    def finish(self, chunks):
+        for g in range(len(self.mine)):
+            for k in range(chunks):
+                self.across(g, k, True).wait_send()
+                self.across(g, k, False).wait_send()
+                self.beyond(g, k).wait_send()
+
+
+class Pace:
+    def __init__(self, steps, every):
+        self.steps, self.every, self.owed = steps, every, 0.0
+
+    def spend(self, time):
+        self.owed += time
+        while self.owed >= self.every:
+            self.owed -= self.every
+            next(self.steps, None)
+
+
+def pair_grads(bounds_ref, causal, q, k, v, g, between):
+    dq = dk = dv = None
+    for keep in halves(q.shape[1]):
+        p = pair_scores(bounds_ref, q, k, keep, causal)
+        dp = dot_nt(jnp.where(keep, g, 0), v)
+        ds = (p * (dp - jnp.sum(p * dp, axis=1, keepdims=True))).astype(jnp.bfloat16)
+        a = jnp.dot(ds, k, preferred_element_type=jnp.float32)
+        b = dot_tt(ds, q)
+        e = dot_tt(p.astype(jnp.bfloat16), g)
+        if dq is None:
+            dq, dk, dv = a, b, e
+        else:
+            dq, dk, dv = jnp.where(keep, a, dq), jnp.where(keep, b, dk), jnp.where(keep, e, dv)
+        between()
+    return [(r * s).astype(jnp.bfloat16) for r, s in ((dq, 0.125), (dk, 0.125), (dv, 1.0))]
+
+
+def middle_body(nz, units, slots, depth, *refs):
+    (bounds, second_low, grad_second, cross_mix, cross_query, cross_keys, cross_values, two_low, first, text_part,
+     proj_part, attended, gain) = refs[:13]
+    weights, feed = refs[13:19], refs[19:21]
+    placed = refs[21:27]
+    text_grad, grad_first, grad_attended, dgain, dbias, sums = refs[27:33]
+    held, (weight_sem, mixed, first_low, grad_ck, grad_cv, twin_k, twin_v, sum_k, sum_v, land_k, land_v) = refs[33:39], refs[39:50]
+    share_sems, stage, stage_sem, scatter = refs[50:54], refs[54], refs[55], refs[56:]
+    here = Place(nz)
+    loads = [pltpu.make_async_copy(w, h, weight_sem.at[i]) for i, (w, h) in enumerate(zip(weights, held))]
+    for cp in loads:
+        cp.start()
+    c_out, c_query, c_key, c_value, w_text, w_out = held
+    steps = scatter_steps(here, units, slots, depth, feed, *scatter)
+    low = jnp.bfloat16
+    width = second_low.shape[1]
+    rows = text_part.shape[0]
+    tiles = [slice(i, i + 256) for i in range(0, width, 256)]
+    share = Share(here, (grad_ck, grad_cv), (twin_k, twin_v), (sum_k, sum_v), (land_k, land_v), *share_sems, width // 2)
+
+    pace = Pace(steps, 32.0 / (len(slots) + depth))
+    spend = pace.spend
+
+    def stored(i):
+        src = stage.at[i % 3, pl.ds(0, placed[i].shape[0])]
+        return pltpu.make_async_copy(src, placed[i], stage_sem.at[i])
+
+    next(steps)
+    loads[0].wait()
+    for n in tiles:
+        mixed[:, n] = dot_nt(second_low[...], c_out[n, :]).astype(low)
+        spend(0.4)
+    for n in tiles:
+        stage[0, n, :] = dot_tt(cross_mix[:, n], second_low[...]).astype(low)
+        spend(0.55)
+    stored(0).start()
+    pairs = width // 128
+    for i in range(pairs):
+        n = slice(i * 128, i * 128 + 128)
+        dq, dk, dv = pair_grads(bounds, False, cross_query[:, n], cross_keys[:, n], cross_values[:, n], mixed[:, n], lambda: spend(0.72))
+        mixed[:, n] = dq
+        grad_ck[:, :, n] = dk.reshape(4, rows, 128)
+        grad_cv[:, :, n] = dv.reshape(4, rows, 128)
+        if i == pairs // 2 - 1:
+            share.send(0)
+    share.send(1)
+    share.forward(0)
+    loads[1].wait()
+    for n in tiles:
+        grad_first[:, n] = dot_nt(mixed[...], c_query[n, :])
+        spend(0.4)
+    share.forward(1)
+    dv, dg, db = norm_grads(first[...], gain[...], grad_first[...])
+    dgain[...] = dg
+    dbias[...] = db
+    dv = grad_second[...] + dv
+    grad_first[...] = dv
+    first_low[...] = dv.astype(low)
+    spend(2.0)
+    loads[5].wait()
+    for n in tiles:
+        grad_attended[:, n] = dot_nt(first_low[...], w_out[n, :]).astype(low)
+        spend(0.4)
+    for n in tiles:
+        stage[1, n, :] = dot_tt(two_low[:, n], mixed[...]).astype(low)
+        spend(0.55)
+    stored(1).start()
+    for n in tiles:
+        stage[2, n, :] = dot_tt(attended[:, n], first_low[...]).astype(low)
+        spend(0.55)
+    stored(2).start()
+    ck = jnp.concatenate([share.collect(0, k) for k in range(2)], axis=1)
+    cv = jnp.concatenate([share.collect(1, k) for k in range(2)], axis=1)
+    for i in (2, 3, 4):
+        loads[i].wait()
+    stored(0).wait()
+    stored(1).wait()
+    for n in tiles:
+        stage[0, n, :] = dot_tt(proj_part[:, n], ck).astype(low)
+        stage[1, n, :] = dot_tt(proj_part[:, n], cv).astype(low)
+        spend(0.7)
+    stored(3).start()
+    stored(4).start()
+    proj = []
+    for n in tiles:
+        proj.append((dot_nt(ck, c_key[n, :]) + dot_nt(cv, c_value[n, :])).astype(low))
+        spend(0.5)
+    proj = jnp.concatenate(proj, axis=1)
+    stored(2).wait()
+    for i in range(0, text_part.shape[1], 256):
+        n = slice(i, i + 256)
+        stage[2, n, :] = dot_tt(text_part[:, n], proj).astype(low)
+        text_grad[:, n] = dot_nt(proj, w_text[n, :])
+        spend(0.7)
+    stored(5).start()
+    for _ in steps:
+        pass
+    share.finish(2)
+    for i in (3, 4, 5):
+        stored(i).wait()
+    total = scatter[0]
+    for u in range(len(units)):
+        sums[u] = total[u, here.z, here.y, here.x].astype(jnp.float32)
+
+
+def middle_back(bounds, near, weights, feed, units, perms, nz, depth=3):
+    slots = make_schedule(perms, nz, lag=depth + 1)
+    second_low, text_part = near[0], near[8]
+    width, rows, text_width = second_low.shape[1], text_part.shape[0], text_part.shape[1]
+    low, wide = jnp.bfloat16, jnp.float32
+    square = jax.ShapeDtypeStruct((width, width), low)
+    outs = [square] * 5 + [jax.ShapeDtypeStruct((text_width, width), low)]
+    outs += [jax.ShapeDtypeStruct(text_part.shape, wide), jax.ShapeDtypeStruct(second_low.shape, wide)]
+    outs += [jax.ShapeDtypeStruct(second_low.shape, low)] + [jax.ShapeDtypeStruct((1, width), wide)] * 2
+    outs += [jax.ShapeDtypeStruct((len(units),) + unit_shape(units), wide)]
+    vmem, any_ = pl.BlockSpec(memory_space=pltpu.VMEM), pl.BlockSpec(memory_space=pl.ANY)
+    part = pltpu.VMEM((rows, width), low)
+    return pl.pallas_call(
+        functools.partial(middle_body, nz, units, slots, depth),
+        out_shape=outs,
+        in_specs=[pl.BlockSpec(memory_space=pltpu.SMEM)] + [vmem] * len(near) + [any_] * 8,
+        out_specs=[any_] * 6 + [vmem] * (len(outs) - 6),
+        scratch_shapes=[pltpu.VMEM(w.shape, low) for w in weights]
+        + [pltpu.SemaphoreType.DMA((6,)), pltpu.VMEM(second_low.shape, low), pltpu.VMEM(second_low.shape, low)]
+        + [pltpu.VMEM((4, rows, width), low)] * 2 + [pltpu.VMEM((2, rows, width), low)] * 2 + [part] * 4
+        + [pltpu.SemaphoreType.DMA((2, 2, 2))] * 2 + [pltpu.SemaphoreType.DMA((2, 2))] * 2
+        + [pltpu.VMEM((3, width, width), low), pltpu.SemaphoreType.DMA((6,))]
+        + scatter_scratch(units, slots, nz),
+        compiler_params=pltpu.CompilerParams(collective_id=5, has_side_effects=True, vmem_limit_bytes=VMEM_LIMIT),
+        name="middle_back",
+    )(bounds, *near, *weights, *feed)
+
+
 eps_norm = 1e-05
 
 
@@ -540,6 +813,7 @@
 
 
 ORDERS = ("zyx", "zxy") * 4 + ("zyx", "yxz", "zxy", "zyx", "xyz", "zxy", "yxz", "zyx", "xyz")
+FEED_ORDERS = ("zyx", "zxy", "zyx", "yxz", "zxy", "zyx", "xyz", "zxy")
 SHORT_ORDERS = ("zyx", "zxy", "zyx", "zxy", "zyx", "zxy", "yxz", "zyx", "xyz")
 
 
@@ -580,6 +854,9 @@
         self.units = [(g, 0, rows, 0, width) for g in range(9)]
         self.units += [(9, 0, rows, k * width, width) for k in range(up)]
         self.units += [(10, k * rows, rows, 0, width) for k in range(down)]
+        feed = self.units[9:]
+        self.feed_units = [(u,) for u in feed]
+        self.near_units = [(u,) for u in self.units[:9]]
         self.orders = [ORDERS[i % len(ORDERS)] for i in range(len(self.units))]
 
     @staticmethod
@@ -606,15 +883,26 @@
         gains = [mixed[:, self.text_rows + i, : own[BLOCKS + i].shape[0]].reshape((-1,)) for i in range(GAINS)]
         return Params(*full, *gains), all_rows.reshape((1, -1, self.width))
 
-    def scatter(self, grads):
+    def middle(self, cross, full, gain, feed):
+        bounds, grad_second, *rest = cross
+        near = [grad_second[0].astype(jnp.bfloat16), grad_second[0]] + [v[0] for v in rest] + [gain[None]]
+        weights = (full.c_out, full.c_query, full.c_key, full.c_value, full.w_text, full.w_out)
+        feed = [v.astype(jnp.bfloat16).reshape((self.nz, 2, 2, 2, -1, v.shape[-1])) for v in feed]
+        units = [tuple((g - 9, *rest) for g, *rest in unit) for unit in self.feed_units]
+        outs = middle_back(bounds[0], near, weights, feed, units, [FEED_ORDERS[i % len(FEED_ORDERS)] for i in range(len(units))], self.nz)
+        dc_out, dc_query, dw_out, dc_key, dc_value, dw_text = outs[:6]
+        return (dc_query, dc_key, dc_value, dc_out, dw_text, dw_out, *[v[None] for v in outs[6:9]], outs[9][0], outs[10][0], outs[11])
+
+    def scatter(self, feed_sums, grads):
         low = [v.astype(jnp.bfloat16) for v in grads]
         shards = self.nz * 8
         rest = jnp.stack([v.reshape((shards, -1)) for v in low[BLOCKS:]], axis=1)
         rest = jnp.pad(rest, ((0, 0), (0, self.rows - self.text_rows - GAINS), (0, self.width - rest.shape[2])))
         low[8] = jnp.concatenate([low[8].reshape((shards, self.text_rows, self.width)), rest], axis=1)
         arrays = [v.reshape((self.nz, 2, 2, 2, -1, v.shape[-1])) for v in low[:BLOCKS]]
-        sums = scatter_grads(arrays, self.units, self.orders, self.nz)
-        *blocks, mixed = deliver(sums, self.units, self.text_rows, [a.shape[4:] for a in arrays])
+        sums = scatter_grads(arrays[:9], self.near_units, SHORT_ORDERS, self.nz)
+        parts = (self.near_units, self.feed_units)
+        *blocks, mixed = deliver((sums, feed_sums), parts, self.text_rows, [a.shape[4:] for a in arrays])
         gains = [mixed[i, : v.shape[0] // shards] for i, v in enumerate(grads[BLOCKS:])]
         return Params(*blocks, *gains)
 
@@ -627,7 +915,33 @@
         full = Params(*[lax.all_gather(v, all_axes(), axis=0, tiled=True) for v in own])
         return full, lax.all_gather(frames, "seq", axis=1, tiled=True)
 
-    def scatter(self, grads):
+    def middle(self, cross, full, gain, feed):
+        bounds, grad_second, cross_mix, cross_query, cross_keys, cross_values, two_low, first, text_part, proj_part, attended = cross
+        low = jnp.bfloat16
+        second_low = grad_second.astype(low)
+        dc_out = outer_sum(cross_mix, second_low)
+        grad_cross_mix = project_back(second_low, full.c_out).astype(low)
+        cq_low, grad_ck, grad_cv = attention_back(False, bounds, cross_query, cross_keys, cross_values, grad_cross_mix)
+        ck_low, cv_low = self.share([grad_ck, grad_cv], 3)
+        dc_key = outer_sum(proj_part, ck_low)
+        dc_value = outer_sum(proj_part, cv_low)
+        grad_proj = (project_back(ck_low, full.c_key) + project_back(cv_low, full.c_value)).astype(low)
+        dw_text = outer_sum(text_part, grad_proj)
+        text_grad = project_back(grad_proj, full.w_text)
+        dc_query = outer_sum(two_low, cq_low)
+        back = jax.vjp(lambda v, s: layer_norm(v, s, jnp.zeros_like(s)), first, gain)[1]
+        two_grad = project_back(cq_low, full.c_query)
+        grad_first_ln, dgain = back(two_grad)
+        grad_first = grad_second + grad_first_ln
+        first_low = grad_first.astype(low)
+        dw_out = outer_sum(attended, first_low)
+        grad_attended = project_back(first_low, full.w_out).astype(low)
+        return (
+            dc_query, dc_key, dc_value, dc_out, dw_text, dw_out, text_grad, grad_first, grad_attended, dgain,
+            jnp.sum(two_grad, axis=(0, 1)), None,
+        )
+
+    def scatter(self, feed_sums, grads):
         return Params(*[lax.psum_scatter(v, all_axes(), scatter_dimension=0, tiled=True) for v in grads])
 
     def share(self, arrays, number):
@@ -686,24 +1000,12 @@
     dw_up = outer_sum(three_low, grad_hidden)
     grad_second_ln, dgain_feed, dbias_feed = norm_three_back(project_back(grad_hidden, full.w_up))
     grad_second = cotangent.astype(jnp.float32) + grad_second_ln
-    second_low = grad_second.astype(low)
-    dc_out = outer_sum(cross_mix, second_low)
-    grad_cross_mix = project_back(second_low, full.c_out).astype(low)
-    cq_low, grad_ck, grad_cv = attention_back(
-        False, cross_bounds, cross_query, cross_keys, cross_values, grad_cross_mix
-    )
-    ck_low, cv_low = wires.share([grad_ck, grad_cv], 3)
-    dc_key = outer_sum(proj_part, ck_low)
-    dc_value = outer_sum(proj_part, cv_low)
-    grad_proj = (project_back(ck_low, full.c_key) + project_back(cv_low, full.c_value)).astype(low)
-    dw_text = outer_sum(text_part, grad_proj)
-    text_grad = project_back(grad_proj, full.w_text)
-    dc_query = outer_sum(normed_two_low, cq_low)
-    grad_first_ln, dgain_cross, dbias_cross = norm_two_back(project_back(cq_low, full.c_query))
-    grad_first = grad_second + grad_first_ln
-    first_low = grad_first.astype(low)
-    dw_out = outer_sum(attended, first_low)
-    grad_attended = project_back(first_low, full.w_out).astype(low)
+    cross = (cross_bounds, grad_second, cross_mix, cross_query, cross_keys, cross_values, normed_two_low, first, text_part, proj_part, attended)
+    middle = wires.middle(cross, full, wide[2], (dw_up, dw_down))
+    (
+        dc_query, dc_key, dc_value, dc_out, dw_text, dw_out, text_grad, grad_first, grad_attended, dgain_cross,
+        dbias_cross, feed_sums,
+    ) = middle
     q_low, grad_k_all, grad_v_all = attention_back(
         True, self_bounds, query_rows, key_all, value_all, grad_attended
     )
@@ -717,10 +1019,11 @@
     grad_frames_ln, dgain_attn, dbias_attn = norm_one_back(grad_normed)
     frames_grad = (grad_first + grad_frames_ln).astype(low)
     sums = wires.scatter(
+        feed_sums,
         Params(
             dw_query, dw_key, dw_value, dw_out, dc_query, dc_key, dc_value, dc_out, dw_text, dw_up, dw_down,
             dgain_attn, dbias_attn, dgain_cross, dbias_cross, dgain_feed, dbias_feed,
-        )
+        ),
     )
     return (block_out, frames_grad, text_grad, *sums)
 

time: 485 us -> 457 us (0.942)
  matrix products: 78.2 us -> 58.1 us
  local copies, waits for them, and re-layouts: 31.1 us -> 17 us
  waiting for transfers between devices: 1.54 us -> 11.1 us
    pallas_call x1 -> x2, Pallas kernels: 1.48 us -> 80.2 us  [the longest x1 78.7 us: middle_back(): pl.pallas_call(functools.partial(middle_body, nz, units, slots, depth), o...]
    pallas_call x1, Pallas kernels: 138 us -> 76.9 us  [scatter_grads(): pl.pallas_call(functools.partial(scatter_body, nz, units, slots, n, depth...]
    unnamed x158 -> x101, local copies, waits for them, and re-layouts: 26 us -> 9.82 us
    dot_general x11 -> x5, matrix products: 31.4 us -> 17.9 us  [outer_sum(): jnp.einsum('gti,gtj->ij', left, right, preferred_element_type=jnp.float32)]
    pallas_call x4 -> x3, Pallas kernels: 46 us -> 34.7 us  [attend_call(): pl.pallas_call(functools.partial(body, causal), grid=(width // 128,), out...]
    pallas_call x2 -> x1, Pallas kernels: 28.8 us -> 18.5 us  [share_sums(): pl.pallas_call(functools.partial(share_body, n, chunk), out_shape=[jax.Sh...]
    all_gather x2, waiting for transfers between devices: 0.16 us -> 9.72 us  [gather(): lax.all_gather(v, all_axes(), axis=0, tiled=True)]
    dot_general x11 -> x5, matrix products: 22 us -> 15.1 us  [project_back(): jnp.einsum('gtj,ij->gti', left, right, preferred_element_type=jnp.float32)]
  transfers between devices with their start and end apart: 2 -> 2, of which waited for: 1 -> 1; matrix products, arithmetic and copies ran while one was open for 6% -> 8% of each run, Pallas kernels for 29% -> 31%
where the time goes in v2:
time: 457 us; the launch traced here: 451 us
  Pallas kernels  333 us (73%)
  matrix products  58.1 us (13%)
  local copies, waits for them, and re-layouts  17 us (4%)
  between operations  16.4 us (4%)
  other arithmetic  14.8 us (3%)
  waiting for transfers between devices  11.1 us (2%)
    pallas_call x1, Pallas kernels, gather_weights(): pl.pallas_call(functools.partial(gather_body, nz, units, slots, n, depth)...  123 us
    pallas_call x1, Pallas kernels, middle_back(): pl.pallas_call(functools.partial(middle_body, nz, units, slots, depth), o...  78.7 us
    pallas_call x1, Pallas kernels, scatter_grads(): pl.pallas_call(functools.partial(scatter_body, nz, units, slots, n, depth...  76.9 us
    pallas_call x3, Pallas kernels, attend_call(): pl.pallas_call(functools.partial(body, causal), grid=(width // 128,), out...  34.7 us
    dot_general x11, matrix products, project(): jnp.einsum('gti,ij->gtj', left, right, preferred_element_type=jnp.float32)  25.1 us
    pallas_call x1, Pallas kernels, share_sums(): pl.pallas_call(functools.partial(share_body, n, chunk), out_shape=[jax.Sh...  18.5 us
    dot_general x5, matrix products, outer_sum(): jnp.einsum('gti,gtj->ij', left, right, preferred_element_type=jnp.float32)  17.9 us
    dot_general x5, matrix products, project_back(): jnp.einsum('gtj,ij->gti', left, right, preferred_element_type=jnp.float32)  15.1 us
  transfers between devices with their start and end apart: 2, of which 1 were waited for; matrix products, arithmetic and copies ran while one was open for 8% of the time, Pallas kernels for 31%

profile of v2, /device:TPU:0, one launch (start us, length us, event | category | flops | bytes accessed | tf_op | source)
XLA Modules:
  0.0 450.7 jit_solution(13485498262843511757)
XLA Ops:
  7.3 0.7 all-gather.3.cloned.1.call-update
  8.0 0.7 all-gather.5.cloned.1.call-update
  10.0 0.8 stack.45
  10.8 1.4 fusion.34.refs_8_
  12.2 122.9 %gather_weights.1 = (bf16[4,2,2,2,32,1024]{5,4,3,2,1,0:T(8,128)(2,1)}, bf16[4,2,2,2,32,1024]{5,4,3,2,1,0:T(8,128)(2,1)}, bf16[4,2,2,2,32,1024]{5,4,3,2,1,0:T(8,1...) custom-call(bf16[32,1024]{1,0:T(8,128)(2,1)} %refs_0_.1, ...), custom_call_target="tpu_custom_call" | custom-call | tf_op jit(solution)/shard_map/gather_weights/pallas_call | solution.py:232
  135.1 1.6 convert_reduce_fusion
  136.8 1.9 multiply_reduce_fusion
  138.8 2.7 slice.56
  141.5 0.9 slice_convert_fusion.3
  142.4 0.7 reshape.745.refs_12_
  143.0 1.6 fusion.36
  145.3 0.2 fusion.19
  145.6 0.5 add_convert_fusion.1
  146.1 0.6 copy-done.37
  146.7 0.6 convolution_convert_fusion.11.q_ref
  147.4 1.5 convolution_convert_fusion.5.v_ref
  149.0 0.2 copy-done.35
  149.2 1.5 convolution_convert_fusion.6.k_ref
  150.8 10.6 %self_attend_body.1.refs_11_ = bf16[160,1024]{1,0:T(8,128)(2,1)S(1)} custom-call(s32[2]{0:T(128)S(1)} %add_bitcast_fusion.1.bounds_ref, bf16[160,1024]{1,0:T(8,128)(2,1)S(1)} %convolution_convert_fusion.11.q_ref, bf16[640,1024]{1,0:T(8,128)(2,1)S(1)} %convolution_convert_fusion.6.k_ref, bf16[640,1024]{1,0:T(8,128)(2,1)S(1)} %convolution_convert_fusion.5.v_ref), custom_call_target="tpu_custom_call" | custom-call | tf_op jit(solution)/shard_map/self_attend_body/pallas_call | solution.py:533
  161.5 0.6 fusion.54
  162.1 0.2 multiply_reduce_fusion.2
  162.6 0.3 copy-done.22
  162.9 0.6 convolution_convert_fusion.9
  163.5 0.7 copy-done.27
  164.2 0.5 convolution_convert_fusion.10.q_ref.refs_4_
  164.8 0.7 convolution_convert_fusion.7.v_ref.refs_6_
  165.5 0.5 copy-done.33
  166.0 0.7 convolution_convert_fusion.8.k_ref.refs_5_
  166.8 7.6 %cross_attend_body.1.refs_3_ = bf16[160,1024]{1,0:T(8,128)(2,1)S(1)} custom-call(s32[2]{0:T(128)S(1)} %add_bitcast_fusion.2.bounds_ref.refs_0_, bf16[160,1024]{1,0:T(8,128)(2,1)S(1)} %convolution_convert_fusion.10.q_ref.refs_4_, bf16[256,1024]{1,0:T(8,128)(2,1)S(1)} %convolution_convert_fusion.8.k_ref.refs_5_, ...), custom_call_target="tpu_custom_call" | custom-call | tf_op jit(solution)/shard_map/cross_attend_body/pallas_call | solution.py:533
  174.4 0.7 dynamic-slice_bitcast_fusion.1.refs_9_
  175.1 0.7 dynamic-slice_bitcast_fusion.refs_10_
  175.8 0.6 fusion.55
  176.5 0.8 copy-done.17
  177.6 11.9 %multiply_convert_fusion = (bf16[160,4096]{1,0:T(8,128)(2,1)}, f32[160,4096]{1,0:T(8,128)}, f32[160,4096]{1,0:T(8,128)}) fusion(bf16[1024,4096]{1,0:T(8,128)(2,1)} %all-gather.3.cloned.1.call-done, f32[1,160,1024]{2,1,0:T(8,128)} %copy-done.17, f32[1024]{0:T(1024)S(1)} %reshape.744, f32[1024]{0:T(1024)S(1)} %reshape.743, f32[160]{0:T(256)S(1)} %fusion.41, ...), kind=kOutput, calls=%fused_computation.5 | convolution fusion | flops 1385594880 | bytes 15607040 | tf_op jit(solution)/shard_map/gti,ij->gtj/dot_general | solution.py:804
  189.5 9.7 %all-gather.5.cloned.1.call-done = bf16[4096,1024]{1,0:T(8,128)(2,1)} async-done(((bf16[128,1024]{1,0:T(8,128)(2,1)}), bf16[4096,1024]{1,0:T(8,128)(2,1)}) %all-gather.5.cloned.1.call-update) | async-done | bytes 8388624 | tf_op jit(solution)/shard_map/all_gather | solution.py:879
  199.2 8.4 %add_convert_fusion = bf16[160,4096]{1,0:T(8,128)(2,1)S(1)} fusion(f32[160,4096]{1,0:T(8,128)} %get-tuple-element.113, f32[160,4096]{1,0:T(8,128)} %get-tuple-element.124, bf16[4096,1024]{1,0:T(8,128)(2,1)} %all-gather.5.cloned.1.call-done, bf16[1,160,1024]{2,1,0:T(8,128)(2,1)S(1)} %copy-done.42), kind=kOutput, calls=%fused_computation.4 | convolution fusion | flops 1351352320 | bytes 15269888 | tf_op jit(solution)/shard_map/gtj,ij->gti/dot_general | solution.py:808
  207.6 5.7 %convolution_convert_fusion.1 = bf16[1024,4096]{1,0:T(8,128)(2,1)} fusion(bf16[160,4096]{1,0:T(8,128)(2,1)S(1)} %add_convert_fusion, f32[1,160,1024]{2,1,0:T(8,128)S(1)} %copy-done.18, f32[1024]{0:T(1024)S(1)} %reshape.744, f32[1024]{0:T(1024)S(1)} %reshape.743, f32[160]{0:T(256)S(1)} %fusion.41, f32[160]{0:T(256)S(1)} %broadcast_multiply_fusion.1), kind=kOutput, calls=%fused_computation.1 | convolution fusion | flops 1347190784 | bytes 10364160 | tf_op jit(solution)/shard_map/gti,gtj->ij/dot_general | solution.py:812
  213.3 3.1 fusion.21
  216.4 0.3 fusion.52
  216.8 1.2 copy-done.23
  218.0 5.6 %convolution_convert_fusion = bf16[4096,1024]{1,0:T(8,128)(2,1)} fusion(bf16[160,4096]{1,0:T(8,128)(2,1)S(1)} %copy-done.23, bf16[1,160,1024]{2,1,0:T(8,128)(2,1)S(1)} %copy-done.42), kind=kOutput, calls=%fused_computation | convolution fusion | flops 1346371584 | bytes 10027008 | tf_op jit(solution)/shard_map/gti,gtj->ij/dot_general | solution.py:812
  223.6 1.1 fusion.51
  224.7 78.7 %middle_back.1 = (bf16[1024,1024]{1,0:T(8,128)(2,1)}, bf16[1024,1024]{1,0:T(8,128)(2,1)}, bf16[1024,1024]{1,0:T(8,128)(2,1)}, bf16[1024,1024]{1,0:T(8,128)(2,1)}...) custom-call(s32[2]{0:T(128)} %copy-done.16, ...), custom_call_target="tpu_custom_call" | custom-call | tf_op jit(solution)/shard_map/middle_back/pallas_call | solution.py:774
  303.4 1.0 copy-done.15
  304.3 16.5 %self_attend_back_body.1 = (bf16[160,1024]{1,0:T(8,128)(2,1)S(1)}, bf16[640,1024]{1,0:T(8,128)(2,1)S(1)}, bf16[640,1024]{1,0:T(8,128)(2,1)S(1)}) custom-call(s32[2]{0:T(128)S(1)} %add_bitcast_fusion.1.bounds_ref, bf16[160,1024]{1,0:T(8,128)(2,1)S(1)} %copy-done.13, bf16[640,1024]{1,0:T(8,128)(2,1)S(1)} %convolution_convert_fusion.6.k_ref, ...), custom_call_target="tpu_custom_call" | custom-call | tf_op jit(solution)/shard_map/self_attend_back_body/pallas_call | solution.py:533
  320.9 1.1 copy-done.8
  322.0 1.1 copy-done.10
  323.0 1.7 fusion.56
  324.7 2.2 convolution_convert_fusion.4
  327.0 1.1 reduce_sum.167
  328.3 18.5 %share_sums.1 = (bf16[160,1024]{1,0:T(8,128)(2,1)S(1)}, bf16[160,1024]{1,0:T(8,128)(2,1)S(1)}) custom-call(bf16[2,2,160,1024]{3,2,1,0:T(8,128)(2,1)S(1)} %bitcast.161, bf16[2,2,160,1024]{3,2,1,0:T(8,128)(2,1)S(1)} %bitcast.162), custom_call_target="tpu_custom_call" | custom-call | tf_op jit(solution)/shard_map/share_sums/pallas_call | solution.py:447
  346.8 2.2 convolution_convert_fusion.3
  349.1 0.8 convolution_add_fusion.1
  349.9 2.1 convolution_convert_fusion.2
  352.1 1.0 fusion.20
  353.2 0.4 fusion.18
  354.1 1.6 pad_maximum_fusion.refs_8_
  355.7 76.9 %scatter_grads.1.refs_0_ = f32[9,32,1024]{2,1,0:T(8,128)} custom-call(bf16[4,2,2,2,32,1024]{5,4,3,2,1,0:T(8,128)(2,1)} %bitcast.185, bf16[4,2,2,2,32,1024]{5,4,3,2,1,0:T(8,128)(2,1)} %bitcast.186, bf16[4,2,2,2,32,1024]{5,4,3,2,1,0:T(8,128)(2,1)} %bitcast.187, bf16[4,2,2,2,32,1024]{5,4,3,2,1,0:T(8,128)(2,1)} %bitcast.182, ...), custom_call_target="tpu_custom_call" | custom-call | tf_op jit(solution)/shard_map/scatter_grads/pallas_call | solution.py:384
  432.6 1.3 copy-done.2
  433.9 1.5 deliver.1
  435.4 0.5 slice_bitcast_fusion
  435.9 1.0 fusion.22
  436.9 5.8 %fusion.9 = bf16[1,160,1024]{2,1,0:T(8,128)(2,1)} fusion(f32[1,160,1024]{2,1,0:T(8,128)S(1)} %copy-done.19, bf16[160,4096]{1,0:T(8,128)(2,1)S(1)} %copy-done.24, bf16[4096,1024]{1,0:T(8,128)(2,1)} %all-gather.5.cloned.1.call-done), kind=kOutput, calls=%fused_computation.39 | convolution fusion | flops 1342504960 | bytes 10682368 | tf_op jit(solution)/shard_map/gti,ij->gtj/dot_general | solution.py:804
  442.7 0.7 copy.54
  (127 shorter events, 2.5 us)
Async XLA Ops:
  7.2 155.4 %copy-start = (bf16[1,256,768]{2,1,0:T(8,128)(2,1)S(1)}, bf16[1,256,768]{2,1,0:T(8,128)(2,1)}, u32[]{:S(2)}) copy-start(bf16[1,256,768]{2,1,0:T(8,128)(2,1)} %param.24) | copy-start | bytes 1179652
  7.2 170.4 %all-gather.3.cloned.1.call-start = ((), (), s32[]{:S(2)}) async-start(), calls=%async_computation | async-start | bytes 8650752 | tf_op jit(solution)/shard_map/all_gather | solution.py:879
  7.9 191.2 %all-gather.5.cloned.1.call-start = ((), (), s32[]{:S(2)}) async-start(), calls=%async_computation.1 | async-start | bytes 8650752 | tf_op jit(solution)/shard_map/all_gather | solution.py:879
  136.7 8.5 %copy-start.21 = (bf16[1,160,1024]{2,1,0:T(8,128)(2,1)S(1)}, bf16[1,160,1024]{2,1,0:T(8,128)(2,1)}, u32[]{:S(2)}) copy-start(bf16[1,160,1024]{2,1,0:T(8,128)(2,1)} %param.22) | copy-start | bytes 983044
  136.8 8.7 %copy-start.25 = (bf16[2,2,160,1024]{3,2,1,0:T(8,128)(2,1)S(1)}, bf16[2,2,160,1024]{3,2,1,0:T(8,128)(2,1)}, u32[]{:S(2)}) copy-start(bf16[2,2,160,1024]{3,2,1,0:T(8,128)(2,1)} %get-tuple-element.61) | copy-start | bytes 3932164
  145.1 1.6 copy-start.37
  145.6 1.9 copy-start.39
  147.3 3.5 copy-start.12
  147.4 1.8 copy-start.35
  150.8 10.7 %copy-start.26 = (bf16[4,2,2,2,32,1024]{5,4,3,2,1,0:T(8,128)(2,1)S(1)}, bf16[4,2,2,2,32,1024]{5,4,3,2,1,0:T(8,128)(2,1)}, u32[]{:S(2)}) copy-start(bf16[4,2,2,2,32,1024]{5,4,3,2,1,0:T(8,128)(2,1)} %get-tuple-element.64) | copy-start | bytes 6291460
  161.4 2.1 copy-start.3
  161.4 1.5 copy-start.22
  161.5 5.3 %copy-start.16 = (s32[2]{0:T(128)}, s32[2]{0:T(128)S(1)}, u32[]{:S(2)}) copy-start(s32[2]{0:T(128)S(1)} %add_bitcast_fusion.2.bounds_ref.refs_0_) | copy-start | bytes 28
  162.1 13.7 %copy-start.20 = (f32[1,160,1024]{2,1,0:T(8,128)}, f32[1,160,1024]{2,1,0:T(8,128)S(1)}, u32[]{:S(2)}) copy-start(f32[1,160,1024]{2,1,0:T(8,128)S(1)} %get-tuple-element.121) | copy-start | bytes 1966084
  162.1 2.1 copy-start.27
  162.6 2.1 copy-start.31
  162.9 1.9 copy-start.34
  164.2 1.9 copy-start.33
  164.7 2.1 copy-start.4
  165.5 9.7 %copy-start.6 = (bf16[256,1024]{1,0:T(8,128)(2,1)}, bf16[256,1024]{1,0:T(8,128)(2,1)S(1)}, u32[]{:S(2)}) copy-start(bf16[256,1024]{1,0:T(8,128)(2,1)S(1)} %convolution_convert_fusion.7.v_ref.refs_6_) | copy-start | bytes 1572868
  166.0 9.8 %copy-start.28 = (bf16[4,2,2,2,32,1024]{5,4,3,2,1,0:T(8,128)(2,1)S(1)}, bf16[4,2,2,2,32,1024]{5,4,3,2,1,0:T(8,128)(2,1)}, u32[]{:S(2)}) copy-start(bf16[4,2,2,2,32,1024]{5,4,3,2,1,0:T(8,128)(2,1)} %get-tuple-element.68) | copy-start | bytes 6291460
  166.8 9.7 %copy-start.7 = (bf16[256,1024]{1,0:T(8,128)(2,1)}, bf16[256,1024]{1,0:T(8,128)(2,1)S(1)}, u32[]{:S(2)}) copy-start(bf16[256,1024]{1,0:T(8,128)(2,1)S(1)} %convolution_convert_fusion.8.k_ref.refs_5_) | copy-start | bytes 1572868
  174.4 1.4 copy-start.5
  176.5 0.8 copy-start.17
  177.5 21.6 %copy-start.42 = (bf16[1,160,1024]{2,1,0:T(8,128)(2,1)S(1)}, bf16[1,160,1024]{2,1,0:T(8,128)(2,1)}, u32[]{:S(2)}) copy-start(bf16[1,160,1024]{2,1,0:T(8,128)(2,1)} %param.23) | copy-start | bytes 983044
  199.2 8.4 %copy-start.18 = (f32[1,160,1024]{2,1,0:T(8,128)S(1)}, f32[1,160,1024]{2,1,0:T(8,128)}, u32[]{:S(2)}) copy-start(f32[1,160,1024]{2,1,0:T(8,128)} %copy-done.17) | copy-start | bytes 1966084
  207.6 5.7 %copy-start.29 = (bf16[1024,4096]{1,0:T(8,128)(2,1)S(1)}, bf16[1024,4096]{1,0:T(8,128)(2,1)}, u32[]{:S(2)}) copy-start(bf16[1024,4096]{1,0:T(8,128)(2,1)} %all-gather.3.cloned.1.call-done) | copy-start | bytes 25165828
  216.4 7.2 %copy-start.30 = (f32[160,1024]{1,0:T(8,128)}, f32[160,1024]{1,0:T(8,128)S(1)}, u32[]{:S(2)}) copy-start(f32[160,1024]{1,0:T(8,128)S(1)} %get-tuple-element.125) | copy-start | bytes 1966084
  216.4 1.6 copy-start.23
  224.7 78.7 %copy-start.13 = (bf16[160,1024]{1,0:T(8,128)(2,1)S(1)}, bf16[160,1024]{1,0:T(8,128)(2,1)}, u32[]{:S(2)}) copy-start(bf16[160,1024]{1,0:T(8,128)(2,1)} %copy-done.12) | copy-start | bytes 983044
  303.4 1.0 copy-start.15
  304.3 18.7 %copy-start.38 = (bf16[4,2,2,2,32,1024]{5,4,3,2,1,0:T(8,128)(2,1)S(1)}, bf16[4,2,2,2,32,1024]{5,4,3,2,1,0:T(8,128)(2,1)}, u32[]{:S(2)}) copy-start(bf16[4,2,2,2,32,1024]{5,4,3,2,1,0:T(8,128)(2,1)} %get-tuple-element.60) | copy-start | bytes 6291460
  320.9 1.1 copy-start.8
  321.9 1.1 copy-start.10
  323.0 5.2 %copy-start.9 = (bf16[640,1024]{1,0:T(8,128)(2,1)S(1)}, bf16[640,1024]{1,0:T(8,128)(2,1)}, u32[]{:S(2)}) copy-start(bf16[640,1024]{1,0:T(8,128)(2,1)} %copy-done.8) | copy-start | bytes 3932164
  323.0 5.2 %copy-start.11 = (bf16[640,1024]{1,0:T(8,128)(2,1)S(1)}, bf16[640,1024]{1,0:T(8,128)(2,1)}, u32[]{:S(2)}) copy-start(bf16[640,1024]{1,0:T(8,128)(2,1)} %copy-done.10) | copy-start | bytes 3932164
  328.3 20.8 %copy-start.32 = (f32[160,1024]{1,0:T(8,128)S(1)}, f32[160,1024]{1,0:T(8,128)}, u32[]{:S(2)}) copy-start(f32[160,1024]{1,0:T(8,128)} %fusion.56) | copy-start | bytes 1966084
  328.3 20.8 %copy-start.36 = (bf16[4,2,2,2,32,1024]{5,4,3,2,1,0:T(8,128)(2,1)S(1)}, bf16[4,2,2,2,32,1024]{5,4,3,2,1,0:T(8,128)(2,1)}, u32[]{:S(2)}) copy-start(bf16[4,2,2,2,32,1024]{5,4,3,2,1,0:T(8,128)(2,1)} %get-tuple-element.62) | copy-start | bytes 6291460
  349.1 3.0 copy-start.40
  352.1 1.5 copy-start.45
  352.1 1.5 copy-start.46
  352.1 2.0 copy-start.41
  355.7 76.9 %copy-start.14 = (f32[8,32,1024]{2,1,0:T(8,128)S(1)}, f32[8,32,1024]{2,1,0:T(8,128)}, u32[]{:S(2)}) copy-start(f32[8,32,1024]{2,1,0:T(8,128)} %get-tuple-element.85.refs_1_) | copy-start | bytes 3145732
  355.7 80.2 %copy-start.43 = (f32[160,1024]{1,0:T(8,128)S(1)}, f32[160,1024]{1,0:T(8,128)}, u32[]{:S(2)}) copy-start(f32[160,1024]{1,0:T(8,128)} %get-tuple-element.69) | copy-start | bytes 1966084
  432.6 1.3 copy-start.2
  433.9 3.0 copy-start.19
  433.9 3.0 copy-start.24
  436.9 5.8 %copy-start.44 = (f32[64,768]{1,0:T(8,128)S(1)}, f32[64,768]{1,0:T(8,128)}, u32[]{:S(2)}) copy-start(f32[64,768]{1,0:T(8,128)} %get-tuple-element.76) | copy-start | bytes 589828
  436.9 6.5 %copy-start.1 = (bf16[1,256,768]{2,1,0:T(8,128)(2,1)S(1)}, bf16[1,256,768]{2,1,0:T(8,128)(2,1)}, u32[]{:S(2)}) copy-start(bf16[1,256,768]{2,1,0:T(8,128)(2,1)} %param.24) | copy-start | bytes 1179652
Sparse Core Ops, SparseCore 0:
  10.9 108.8 all-gather.2
  122.7 76.4 all-gather.4
